TPU v7x, 32 devices: a whole 2x2x4 slice. The times are simulated.
32 devices in a mesh: owner: 8 (over z, core), tensor: 4 (over y, x).
Axes of the slice: x: 2, y: 2, z: 4, core: 2. Of those that a mesh axis runs over, the one named last changes fastest.
Arguments:
- mixer_input: bfloat16 [8192, 2, 8192], P('owner', None, 'tensor'), may hold values from -6 to 6
- step_raw: float32 [8192, 128], P('owner', 'tensor'), may hold values from -7 to 5
- decay_rate: float32 [128], P('tensor'), may hold values from 0.005 to 0.5
- skip_gain: float32 [128], P('tensor'), may hold values from 0.5 to 2
- state_proj: bfloat16 [8192, 2, 4, 256], P('owner'), may hold values from -1.5 to 1.5
- queries: bfloat16 [8192, 4096], P('owner', 'tensor'), may hold values from -256 to 256
- suffix_kv: bfloat16 [8192, 2, 4, 128], P('owner'), may hold values from -6 to 6
- state_pool: bfloat16 [32, 128, 64, 256], P('owner', 'tensor'), may hold values from -1.5 to 1.5
- page_pool: bfloat16 [128, 128, 2, 4, 128], P('owner'), may hold values from -6 to 6
- norm_gain: float32 [8192], P('tensor'), may hold values from 0.1 to 1.9
- hit_owner: int32 [32, 1], replicated, may hold values from 0 to 7; in each aligned block of 4 rows (0 to 3, 4 to 7, ...) at most 2 rows name the same one
- hit_slot: int32 [32], replicated, may hold values from 0 to 3
- page_owner: int32 [32, 16, 1], replicated, may hold values from 0 to 7; in each aligned block of 64 rows (0 to 63, 64 to 127, ..., all dimensions but the last counted through in order) at most 12 rows name the same one
- page_slot: int32 [32, 16], replicated, may hold values from 0 to 15
- prefix_len: int32 [32], replicated, may hold values from 256 to 2048, as said below
- suffix_len: int32 [32], replicated, may hold values from 64 to 256, as said below
Outputs:
- mamba_out: bfloat16 [8192, 8192], P('owner', 'tensor')
- attn_out: bfloat16 [8192, 4096], P('owner', 'tensor')
Inputs may be any that keep to these rules, and one draw needn't show every extreme that they name: `hit_owner`: the 4 requests on one index of owner name one owner at most 2 times, and some index reaches it. `page_owner`: of the 64 list entries of the requests on one index of owner, at most 12 name one owner, and some index reaches it. `prefix_len`: a multiple of 256; request 0 has 2048. `suffix_len`: request 0 has 256.
All inputs are finite; a program needn't handle non-finite values.
Results may differ from a plain program's by a relative error of at most 0.0045.
Values may be sent and summed in bfloat16 or wider, within the bound.
No kernel may reach another device: no remote copies, remote signals or barrier semaphores. Data moves between devices by JAX's collectives and lax.ppermute only.
A program may use at most 256 MiB of HBM per device.

v0:
```python
import functools
import math

import jax
import jax.numpy as jnp
import numpy as np
from jax import lax
from jax.experimental import pallas as pl
from jax.experimental.pallas import tpu as pltpu
from jax.sharding import PartitionSpec as P

SSM_HEAD_TOTAL = 128
MHDIM = 64
STATE = 256
GROUPS = 4
QHEADS = 32
KVHEADS = 4
HD = 128
PAGE = 128
SPAN = 128
SUF = 256
MAXP = 16
SLOTS_DEV = 4
PAGES_DEV = 16

EPSILON = 1e-05
NEG_FILL = -1e30
LAG = 2
HOP_STEPS = 2
FREE_STEPS = 7
VMEM = 48 * 1024 * 1024
SMALL_VMEM = 58 * 1024 * 1024

NT = (((1,), (1,)), ((), ()))
TN = (((0,), (0,)), ((), ()))


def mm(a, b, dims=(((1,), (0,)), ((), ()))):
    return lax.dot_general(a, b, dims, preferred_element_type=jnp.float32)


def route_kernel(chips, per_chip, reqs_per_chip, cap, ids_ref, here_ref, out_ref, need_ref, own_ref, tab_ref, code_ref):
    states = chips * per_chip
    chip_here = here_ref[0] // 2
    core_here = here_ref[0] % 2

    def clear(s, carry):
        need_ref[s] = 0
        return carry

    lax.fori_loop(0, states, clear, 0)

    def mark(r, carry):
        s = ids_ref[r]
        need_ref[s] = need_ref[s] | (1 << (r // reqs_per_chip))
        return carry

    lax.fori_loop(0, chips * reqs_per_chip, mark, 0)

    def put(base, length, row, from_ref):
        def one(t, carry):
            spot = jnp.clip(base + t, 0, 2 * chips * cap - 1)
            out_ref[row * cap + t] = jnp.where(t < length, from_ref[spot], states)
            return carry

        lax.fori_loop(0, cap, one, 0)

    steps = jnp.int32(0)
    for up in (True, False):
        before = jnp.int32(0)
        sent = jnp.int32(0)
        came = jnp.int32(0)
        for place in range(chips - 1):
            chip = place if up else chips - 1 - place
            base = ((0 if up else chips) + place) * cap

            def wanted(s, further=0, chip=chip, up=up):
                if up:
                    return (need_ref[s] >> (chip + 1 + further)) != 0
                return (need_ref[s] & ((1 << max(chip - further, 0)) - 1)) != 0

            count = jnp.int32(0)
            for far in (True, False):

                def own(i, n, far=far, chip=chip, wanted=wanted):
                    s = chip * per_chip + i
                    own_ref[n] = s
                    beyond = wanted(s, 1)
                    take = beyond if far else wanted(s) & jnp.logical_not(beyond)
                    return n + take.astype(jnp.int32)

                count = lax.fori_loop(0, per_chip, own, count)

            def fill(t, used, base=base, count=count):
                s = jnp.where(used < count, own_ref[used], states)
                tab_ref[base + t] = s
                code_ref[base + t] = s
                return jnp.minimum(used + 1, count)

            def forward(j, carry, base=base, wanted=wanted, fill=fill):
                t, used = carry
                s = tab_ref[base - cap + j]
                take = (s < states) & wanted(jnp.minimum(s, states - 1))
                later = jnp.where(take, jnp.maximum(t, j + LAG), t)
                used = lax.fori_loop(t, later, fill, used)
                tab_ref[base + later] = s
                code_ref[base + later] = states + 1 + j
                return later + take.astype(jnp.int32), used

            def idle(t, carry, base=base):
                tab_ref[base + t] = states
                code_ref[base + t] = states
                return carry

            lax.fori_loop(0, HOP_STEPS * place, idle, 0)
            t, used = jnp.int32(HOP_STEPS * place), jnp.int32(0)
            if place:
                t, used = lax.fori_loop(0, before, forward, (t, used))
            end = t + count - used
            lax.fori_loop(t, end, fill, used)
            before = end
            sent = jnp.where(chip_here == chip, end, sent)
            came = jnp.where(chip_here == (chip + 1 if up else chip - 1), end, came)
            steps = jnp.maximum(steps, end)
        here = chip_here if up else chips - 1 - chip_here
        side = 0 if up else chips

        @pl.when(core_here == (0 if up else 1))
        def _(here=here, side=side, sent=sent, came=came):
            put((side + here) * cap, sent, 0, code_ref)
            put((side + here - 1) * cap, came, 1, tab_ref)

        arrived = came if up else jnp.where(core_here == 0, arrived, came)

    out_ref[2 * cap] = steps
    mine = reqs_per_chip // 2
    asked = [here_ref[0] * mine + r for r in range(mine)] + [(here_ref[0] ^ 1) * mine + r for r in range(mine)]
    for k, request in enumerate(asked):
        state = ids_ref[request]
        out_ref[2 * cap + 3 + mine + k] = jnp.where(state // per_chip == chip_here, state, -1)

    def look(t, carry):
        came_now = out_ref[cap + t]
        for k, request in enumerate(asked):

            @pl.when(ids_ref[request] == came_now)
            def _(k=k):
                out_ref[2 * cap + 3 + mine + k] = states + 1 + t

        return carry

    lax.fori_loop(0, arrived, look, 0)
    found = jnp.int32(0)
    for here_now in (True, False):
        for r in range(mine):
            out_ref[2 * cap + 2 + found] = r
            found += ((out_ref[2 * cap + 3 + mine + r] >= 0) == here_now).astype(jnp.int32)
        if here_now:
            out_ref[2 * cap + 1] = found


def route(state_ids, owner, chips, per_chip, reqs_per_chip):
    cap = chips * per_chip + (LAG + HOP_STEPS) * chips + 8
    smem = pl.BlockSpec(memory_space=pltpu.SMEM)
    table = pl.pallas_call(
        functools.partial(route_kernel, chips, per_chip, reqs_per_chip, cap),
        out_shape=jax.ShapeDtypeStruct((2 * cap + 4 + 2 * reqs_per_chip,), jnp.int32),
        in_specs=[smem, smem],
        out_specs=smem,
        scratch_shapes=[
            pltpu.SMEM((chips * per_chip,), jnp.int32),
            pltpu.SMEM((2 * per_chip,), jnp.int32),
            pltpu.SMEM((2 * chips * cap,), jnp.int32),
            pltpu.SMEM((2 * chips * cap,), jnp.int32),
        ],
        name="route_states",
    )(state_ids, owner.reshape(1))
    return table, cap


ANYWHERE = pl.BlockSpec(memory_space=pl.ANY)
IN_HBM = pl.BlockSpec(memory_space=pltpu.HBM)
PIECES = 4


def piece_of(ref, k):
    rows = ref.shape[0] // PIECES
    return ref.at[pl.ds(k * rows, rows)]


def start_from(code, states, owner, pool_ref, near_ref, came_refs, late_ref, dst, sems):
    def start(ref):
        for k in range(PIECES):
            pltpu.make_async_copy(piece_of(ref, k), piece_of(dst, k), sems.at[k]).start()

    if pool_ref is not None:
        own = (code >= 0) & (code < states)
        slot = code % SLOTS_DEV

        @pl.when(own & (code // SLOTS_DEV == owner))
        def _():
            start(pool_ref.at[slot])

        @pl.when(own & (code // SLOTS_DEV != owner))
        def _():
            start(near_ref.at[slot])

    step = code - states - 1
    for k, ref in enumerate(came_refs):

        @pl.when(step == k)
        def _(ref=ref):
            start(ref)

    if late_ref is not None:

        @pl.when(step >= len(came_refs))
        def _():
            start(late_ref.at[step - len(came_refs)])


def pass_on(src, dst, sems):
    for k in range(PIECES):
        pltpu.make_async_copy(piece_of(dst, k), piece_of(src, k), sems.at[k]).wait()
        pltpu.make_async_copy(piece_of(src, k), piece_of(dst, k), sems.at[k]).start()


def finish(src, dst, sems):
    for k in range(PIECES):
        pltpu.make_async_copy(piece_of(src, k), piece_of(dst, k), sems.at[k]).wait()


def take_kernel(states, steps, late, here_ref, table_ref, step_ref, pool_ref, near_ref, *rest):
    sends, (item_ref, sem) = rest[-2 - steps : -2], rest[-2:]
    came_refs = rest[: -2 - steps]
    late_ref = None
    if late:
        came_refs, late_ref = came_refs[:-1], came_refs[-1]
    codes = [table_ref[step_ref[0] + t] for t in range(steps)]
    for t in range(steps):
        start_from(
            codes[t], states, here_ref[0], pool_ref, near_ref, came_refs, late_ref, item_ref.at[t], sem.at[t]
        )
    for act in (pass_on, finish):
        for t in range(steps):

            @pl.when(codes[t] != states)
            def _(t=t):
                act(item_ref.at[t], sends[t], sem.at[t])


def take(states, steps, here, table, step, pool, near, came, late=None):
    item = jax.ShapeDtypeStruct(pool.shape[1:], pool.dtype)
    came = list(came) + ([] if late is None else [late])
    return pl.pallas_call(
        functools.partial(take_kernel, states, steps, late is not None),
        grid_spec=pltpu.PrefetchScalarGridSpec(
            num_scalar_prefetch=3,
            grid=(1,),
            in_specs=[IN_HBM] * (2 + len(came)),
            out_specs=[IN_HBM] * steps,
            scratch_shapes=[
                pltpu.VMEM((steps,) + pool.shape[1:], pool.dtype),
                pltpu.SemaphoreType.DMA((steps, PIECES)),
            ],
        ),
        out_shape=[item] * steps,
        compiler_params=pltpu.CompilerParams(vmem_limit_bytes=SMALL_VMEM),
        name="take_states",
    )(here, table, step, pool, near, *came)


def keep_kernel(fixed, step_ref, got_ref, _late_in, late_ref, item_ref, sem):
    spot = late_ref.at[step_ref[0] - fixed]
    for k in range(PIECES):
        pltpu.make_async_copy(piece_of(got_ref, k), piece_of(item_ref, k), sem.at[k]).start()
    pass_on(item_ref, spot, sem)
    finish(item_ref, spot, sem)


def keep(fixed, step, got, late):
    return pl.pallas_call(
        functools.partial(keep_kernel, fixed),
        grid_spec=pltpu.PrefetchScalarGridSpec(
            num_scalar_prefetch=1,
            grid=(1,),
            in_specs=[IN_HBM, IN_HBM],
            out_specs=IN_HBM,
            scratch_shapes=[pltpu.VMEM(got.shape, got.dtype), pltpu.SemaphoreType.DMA((PIECES,))],
        ),
        out_shape=jax.ShapeDtypeStruct(late.shape, late.dtype),
        input_output_aliases={2: 0},
        compiler_params=pltpu.CompilerParams(vmem_limit_bytes=SMALL_VMEM),
        name="keep_state",
    )(step, got, late)


def blank_kernel(here_ref, out_ref):
    pass


def blank(here, shape, dtype):
    return pl.pallas_call(
        blank_kernel,
        in_specs=[pl.BlockSpec(memory_space=pltpu.SMEM)],
        out_specs=IN_HBM,
        out_shape=jax.ShapeDtypeStruct(shape, dtype),
        compiler_params=pltpu.CompilerParams(vmem_limit_bytes=SMALL_VMEM),
        name="room",
    )(here)


def pick_kernel(states, cap, count, table_ref, *rest):
    came_refs, late_ref = rest[:-4], rest[-4]
    out_ref, item_ref, sem = rest[-3:]
    codes = [table_ref[2 * cap + 3 + 2 * count + r] for r in range(count)]
    for r in range(count):

        @pl.when(codes[r] > states)
        def _(r=r):
            start_from(codes[r], states, -1, None, None, came_refs, late_ref, item_ref.at[r], sem.at[r])

    for act in (pass_on, finish):
        for r in range(count):

            @pl.when(codes[r] > states)
            def _(r=r):
                act(item_ref.at[r], out_ref.at[r], sem.at[r])


def pick(states, cap, count, table, came, late):
    shape = (count,) + late.shape[1:]
    return pl.pallas_call(
        functools.partial(pick_kernel, states, cap, count),
        grid_spec=pltpu.PrefetchScalarGridSpec(
            num_scalar_prefetch=1,
            grid=(1,),
            in_specs=[IN_HBM] * (len(came) + 1),
            out_specs=IN_HBM,
            scratch_shapes=[
                pltpu.VMEM(shape, late.dtype),
                pltpu.SemaphoreType.DMA((count, PIECES)),
            ],
        ),
        out_shape=jax.ShapeDtypeStruct(shape, late.dtype),
        compiler_params=pltpu.CompilerParams(vmem_limit_bytes=SMALL_VMEM),
        name="pick_states",
    )(table, *came, late)


def mamba_pre_kernel(
    heads,
    live_ref,
    first_ref,
    mix_ref,
    b_ref,
    c_ref,
    step_ref,
    decay_ref,
    skip_ref,
    spread_ref,
    split_ref,
    _pre_in,
    _z_in,
    _e_in,
    pre_ref,
    z_ref,
    e_ref,
    bs_ref,
    end_ref,
):
    block = pl.program_id(1)
    request = first_ref[0] + pl.program_id(0)
    copies = SPAN // heads
    row = lax.broadcasted_iota(jnp.int32, (SPAN, SPAN), 0)
    lane = lax.broadcasted_iota(jnp.int32, (SPAN, SPAN), 1)
    lower = row >= lane
    left = lane < MHDIM

    def three_way(value):
        high = value.astype(jnp.bfloat16)
        rest = value - high.astype(jnp.float32)
        middle = rest.astype(jnp.bfloat16)
        low = (rest - middle.astype(jnp.float32)).astype(jnp.bfloat16)
        high, middle, low = (v.astype(jnp.float32) for v in (high, middle, low))
        kept = jnp.where(
            lane < heads,
            high,
            jnp.where(lane < 2 * heads, middle, jnp.where(lane < 3 * heads, low, 0.0)),
        )
        return kept.astype(jnp.bfloat16)

    @pl.when((block == 0) | (live_ref[request] > SPAN))
    def _():
        raw = step_ref[...]
        rate_row = jnp.maximum(raw, 0.0) + jnp.log1p(jnp.exp(-jnp.abs(raw)))
        upper = jnp.where(row <= lane, 1.0, 0.0)
        cum_row = lax.dot_general(
            -rate_row * decay_ref[...],
            upper,
            (((1,), (0,)), ((), ())),
            precision=lax.Precision.HIGHEST,
            preferred_element_type=jnp.float32,
        )
        cum = jnp.concatenate([cum_row] * copies, axis=0).T
        rate_col = jnp.concatenate([rate_row] * copies, axis=0).T

        both = mm(split_ref[...], mix_ref[...].reshape(2 * SPAN, heads * MHDIM))
        z_ref[...] = both[SPAN:].astype(jnp.bfloat16)
        x = both[:SPAN]
        x_half = x.astype(jnp.bfloat16)
        b = b_ref[...]
        c = c_ref[...]
        cross = mm(c, b, NT)

        def weights(h):
            fall = cum[:, h : h + 1] - cum_row[h : h + 1, :]
            fade = jnp.exp(jnp.where(lower, fall, NEG_FILL))
            return (cross * fade * rate_row[h : h + 1, :]).astype(jnp.bfloat16)

        for pair in range(heads // 2):
            cols = slice(pair * 2 * MHDIM, (pair + 1) * 2 * MHDIM)
            xp = x_half[:, cols]
            zero = jnp.zeros_like(xp)
            stacked = jnp.concatenate([jnp.where(left, xp, zero), jnp.where(left, zero, xp)], axis=0)
            w = jnp.concatenate([weights(2 * pair), weights(2 * pair + 1)], axis=1)
            pre_ref[:, cols] = mm(w, stacked) + skip_ref[:, cols] * x[:, cols]

        @pl.when(block == 0)
        def _():
            end = cum[SPAN - 1 : SPAN, :]
            tail = jnp.exp(end - cum) * rate_col
            scaled = (mm(three_way(tail), spread_ref[...]) * x).astype(jnp.bfloat16)
            bs_ref[...] = mm(scaled, b, TN).astype(jnp.bfloat16)
            end_ref[...] = jnp.broadcast_to(end, end_ref.shape)
            e_ref[...] = three_way(jnp.exp(cum))

        @pl.when(block == 1)
        def _():
            e_half = three_way(jnp.exp(cum))
            carried = mm(c, bs_ref[...], NT)
            pre_ref[...] += mm(e_half, spread_ref[...]) * carried
            e_ref[...] = three_way(jnp.exp(cum + end_ref[0:1, :]))


def mamba_pre(heads, first, count, live, here, mixed, b_rows, c_rows, step_row, decay, skip, spread, split, carry):
    width = heads * MHDIM
    rows = b_rows.shape[0]

    def at(r, k, *_):
        return ((first + r) * 2 + k, 0)

    def fixed(r, k, *_):
        return (0, 0)

    blocks = count * 2
    outs = [
        jax.ShapeDtypeStruct((rows, width), jnp.float32),
        jax.ShapeDtypeStruct((rows, width), jnp.bfloat16),
        jax.ShapeDtypeStruct((rows, 128), jnp.bfloat16),
    ]
    if carry is None:
        carry = tuple(jnp.zeros((16, 128), jnp.float32) for _ in outs)
        aliases = {}
    else:
        aliases = {10: 0, 11: 1, 12: 2}
    return pl.pallas_call(
        functools.partial(mamba_pre_kernel, heads),
        grid_spec=pltpu.PrefetchScalarGridSpec(
            num_scalar_prefetch=2,
            grid=(count, 2),
            in_specs=[
                pl.BlockSpec((SPAN, 2, width), lambda r, k, *_: ((first + r) * 2 + k, 0, 0)),
                pl.BlockSpec((SPAN, STATE), at),
                pl.BlockSpec((SPAN, STATE), at),
                pl.BlockSpec((heads, SPAN), lambda r, k, *_: (0, (first + r) * 2 + k)),
                pl.BlockSpec((heads, SPAN), fixed),
                pl.BlockSpec((1, width), fixed),
                pl.BlockSpec((128, width), fixed),
                pl.BlockSpec((2 * SPAN, 2 * SPAN), fixed),
                ANYWHERE,
                ANYWHERE,
                ANYWHERE,
            ],
            out_specs=[
                pl.BlockSpec((SPAN, width), at),
                pl.BlockSpec((SPAN, width), at),
                pl.BlockSpec((SPAN, 128), at),
            ],
            scratch_shapes=[
                pltpu.VMEM((width, STATE), jnp.bfloat16),
                pltpu.VMEM((8, 128), jnp.float32),
            ],
        ),
        out_shape=outs,
        input_output_aliases=aliases,
        compiler_params=pltpu.CompilerParams(vmem_limit_bytes=VMEM),
        cost_estimate=pl.CostEstimate(
            flops=blocks * heads * 40 * SPAN * SPAN * MHDIM,
            bytes_accessed=blocks * SPAN * width * 10,
            transcendentals=blocks * heads * SPAN * SPAN,
        ),
        name="mamba_pre",
    )(live, here + first, mixed, b_rows, c_rows, step_row, decay, skip, spread, split, *carry)


def mamba_post_kernel(
    heads,
    whole_group,
    count,
    cap,
    states,
    fixed,
    late,
    here_ref,
    table_ref,
    live_ref,
    *rest,
):
    outs = 1 if whole_group else 2
    pool_ref, near_ref, *came_refs, late_ref, other_ref = rest[: fixed + 4]
    c_ref, pre_ref, z_ref, e_ref, spread_ref, gain_ref, *rest = rest[fixed + 4 :]
    out_refs = rest[outs : 2 * outs]
    stage_refs = rest[2 * outs : 3 * outs]
    state_ref, sem, out_sem = rest[-3:]
    i = pl.program_id(0)
    width = heads * MHDIM
    owner = here_ref[0]
    here_now = table_ref[2 * cap + 1]
    active = count - here_now if late else here_now

    def put(i, r):
        rows = pl.ds(pl.multiple_of(r * SUF, SUF), SUF)
        return [
            pltpu.make_async_copy(stage.at[i % 2], out.at[rows], out_sem.at[k, i % 2])
            for k, (stage, out) in enumerate(zip(stage_refs, out_refs))
        ]

    def fetch(i):
        r = post_request(cap, count, late, i, table_ref)
        code = table_ref[2 * cap + 3 + count + r]
        slot = i % 2
        start_from(
            code, states, owner, pool_ref, near_ref, came_refs, late_ref, state_ref.at[slot], sem.at[slot]
        )
        if late:

            @pl.when(code < 0)
            def _():
                for k in range(PIECES):
                    pltpu.make_async_copy(
                        piece_of(other_ref.at[r], k), piece_of(state_ref.at[slot], k), sem.at[slot, k]
                    ).start()

    @pl.when((i == 0) & (i < active))
    def _():
        fetch(i)

    @pl.when(i + 1 < active)
    def _():
        fetch(i + 1)

    @pl.when(i < active)
    def _():
        r = post_request(cap, count, late, i, table_ref)
        finish(pool_ref.at[0], state_ref.at[i % 2], sem.at[i % 2])
        carried = mm(c_ref[...], state_ref[i % 2], NT)
        summed = pre_ref[...] + mm(e_ref[...], spread_ref[...]) * carried
        z = z_ref[...].astype(jnp.float32)
        gated = summed * (z / (1.0 + jnp.exp(-z)))
        square = jnp.sum(gated * gated, axis=1, keepdims=True)

        @pl.when(i >= 2)
        def _():
            for copy in put(i, 0):
                copy.wait()

        if whole_group:
            norm = lax.rsqrt(square / width + EPSILON)
            live = lax.broadcasted_iota(jnp.int32, (SUF, 1), 0) < live_ref[owner * count + r]
            stage_refs[0][i % 2] = jnp.where(live, gated * norm * gain_ref[...], 0.0).astype(jnp.bfloat16)
        else:
            stage_refs[0][i % 2] = gated
            stage_refs[1][i % 2] = jnp.broadcast_to(square, (SUF, 128))
        for copy in put(i, r):
            copy.start()

        @pl.when(i == active - 1)
        def _():
            for copy in put(i, 0):
                copy.wait()

            @pl.when(i >= 1)
            def _():
                for copy in put(i - 1, 0):
                    copy.wait()


def post_request(cap, count, late, i, table_ref):
    here_now = table_ref[2 * cap + 1]
    if late:
        spot = here_now + jnp.minimum(i, jnp.maximum(count - here_now - 1, 0))
    else:
        spot = jnp.minimum(i, jnp.maximum(here_now - 1, 0))
    return table_ref[2 * cap + 2 + jnp.minimum(spot, count - 1)]


def mamba_post(
    heads, whole_group, cap, states, here, table, live, pool, near, came, late_room, other, c_rows, pre, z, e3, spread, gain, carry
):
    width = heads * MHDIM
    rows = c_rows.shape[0]
    count = rows // SUF
    late = carry is not None
    held = len(came)

    def at(i, here_ref, table_ref, *_):
        return (post_request(cap, count, late, i, table_ref), 0)

    def fixed(i, *_):
        return (0, 0)

    out_shape = [jax.ShapeDtypeStruct((rows, width), jnp.bfloat16 if whole_group else jnp.float32)]
    if not whole_group:
        out_shape.append(jax.ShapeDtypeStruct((rows, 128), jnp.float32))
    aliases = {}
    if late:
        aliases = {3 + held + 10 + k: k for k in range(len(out_shape))}
    else:
        carry = [jnp.zeros((16, 128), jnp.float32)] * len(out_shape)
        other = late_room
    return pl.pallas_call(
        functools.partial(mamba_post_kernel, heads, whole_group, count, cap, states, held, late),
        grid_spec=pltpu.PrefetchScalarGridSpec(
            num_scalar_prefetch=3,
            grid=(count,),
            in_specs=[IN_HBM] * (held + 4)
            + [
                pl.BlockSpec((SUF, STATE), at),
                pl.BlockSpec((SUF, width), at),
                pl.BlockSpec((SUF, width), at),
                pl.BlockSpec((SUF, 128), at),
                pl.BlockSpec((128, width), fixed),
                pl.BlockSpec((1, width), fixed),
            ]
            + [ANYWHERE] * len(out_shape),
            out_specs=[IN_HBM] * len(out_shape),
            scratch_shapes=[pltpu.VMEM((2, SUF) + out.shape[1:], out.dtype) for out in out_shape]
            + [
                pltpu.VMEM((2, width, STATE), jnp.bfloat16),
                pltpu.SemaphoreType.DMA((2, PIECES)),
                pltpu.SemaphoreType.DMA((len(out_shape), 2)),
            ],
        ),
        out_shape=out_shape,
        input_output_aliases=aliases,
        compiler_params=pltpu.CompilerParams(vmem_limit_bytes=VMEM),
        cost_estimate=pl.CostEstimate(
            flops=2 * rows * width * STATE,
            bytes_accessed=rows * width * 6,
            transcendentals=rows * width,
        ),
        name="mamba_post",
    )(here, table, live, pool, near, *came, late_room, other, c_rows, pre, z, e3, spread, gain, *carry)


def attend_kernel(
    qheads,
    chips,
    first_ref,
    pages_ref,
    prefix_ref,
    live_ref,
    q_ref,
    ks_ref,
    vs_ref,
    *rest,
):
    parts = rest[: 4 * chips - 2]
    out_ref, kv_ref, s_ref, top_ref, total_ref, mixed_ref, sem = rest[4 * chips - 1 :]
    request = first_ref[0]
    owner = first_ref[1]
    scale = math.log2(math.e) / math.sqrt(HD)
    pairs = prefix_ref[request] // (2 * PAGE)
    half = pl.program_id(0)
    start = half * SPAN
    live = live_ref[request]

    def columns(h):
        return slice(h * HD, (h + 1) * HD)

    @pl.when(half == 0)
    def _():
        def begin(p, carry):
            page = pages_ref[request * MAXP + p]
            giver = page // PAGES_DEV
            core = owner % 2
            away = giver // 2 - owner // 2
            ahead = jnp.where(core == 0, -away, away)
            which = jnp.where(ahead >= 0, ahead, chips - 1 - ahead)
            carrier = jnp.where(ahead >= 0, core, 1 - core)
            which = 2 * which + ((giver % 2) ^ carrier)
            spot = page % PAGES_DEV

            def fetch(low, high):
                if high - low == 1:
                    pltpu.make_async_copy(parts[low].at[spot], kv_ref.at[p + 2], sem).start()
                    return
                middle = (low + high) // 2

                @pl.when(which < middle)
                def _():
                    fetch(low, middle)

                @pl.when(which >= middle)
                def _():
                    fetch(middle, high)

            fetch(0, len(parts))
            return carry

        def end(p, carry):
            pltpu.make_async_copy(parts[0].at[0], kv_ref.at[p + 2], sem).wait()
            return carry

        lax.fori_loop(0, 2 * pairs, begin, 0)
        for page in range(2):
            at = slice(page * PAGE, (page + 1) * PAGE)
            kv_ref[page, 0] = ks_ref[at, :]
            kv_ref[page, 1] = vs_ref[at, :]
        lax.fori_loop(0, 2 * pairs, end, 0)

    @pl.when(start < live)
    def _():
        odd = pairs % 2

        def block(first, pages, kv):
            return kv_ref[pl.ds(first, pages), kv].reshape(pages * PAGE, HD)

        def place(i):
            return 2 + 2 * odd + 4 * i

        def fold(s, act):
            return functools.reduce(act, [s[:, k : k + HD] for k in range(0, s.shape[1], HD)])

        def first_scores(pages):
            keys = block(0, pages, 0)
            row = lax.broadcasted_iota(jnp.int32, (SPAN, pages * PAGE), 0) + start
            lane = lax.broadcasted_iota(jnp.int32, (SPAN, pages * PAGE), 1)
            allowed = (row >= lane) | (lane >= SUF)
            for h in range(qheads):
                s = jnp.where(allowed, mm(q_ref[:, columns(h)], keys, NT), NEG_FILL)
                s_ref[0, h, :, : pages * PAGE] = s
                top_ref[h] = fold(s, jnp.maximum)

        def scores(i, carry):
            keys = block(place(i), 4, 0)
            for h in range(qheads):
                s = mm(q_ref[:, columns(h)], keys, NT)
                s_ref[i + 1, h] = s
                top_ref[h] = jnp.maximum(top_ref[h], fold(s, jnp.maximum))
            return carry

        def weigh(h, s, values):
            top = jnp.concatenate([top_ref[h]] * (s.shape[1] // HD), axis=1)
            probs = jnp.exp2((s - top) * scale)
            return fold(probs, jnp.add), mm(probs.astype(jnp.bfloat16), values)

        def first_values(pages):
            rows = block(0, pages, 1)
            for h in range(qheads):
                total_ref[h], mixed_ref[h] = weigh(h, s_ref[0, h, :, : pages * PAGE], rows)

        def values(i, carry):
            rows = block(place(i), 4, 1)
            for h in range(qheads):
                total, mixed = weigh(h, s_ref[i + 1, h], rows)
                total_ref[h] += total
                mixed_ref[h] += mixed
            return carry

        def first_block(act):
            @pl.when(odd == 0)
            def _():
                act(2)

            @pl.when(odd == 1)
            def _():
                act(4)

        first_block(first_scores)
        lax.fori_loop(0, pairs // 2, scores, 0)
        for h in range(qheads):
            top_ref[h] = jnp.broadcast_to(jnp.max(top_ref[h], axis=1, keepdims=True), (SPAN, HD))
        first_block(first_values)
        lax.fori_loop(0, pairs // 2, values, 0)
        keep_row = lax.broadcasted_iota(jnp.int32, (SPAN, 1), 0) + start < live
        for h in range(qheads):
            total = jnp.sum(total_ref[h], axis=1, keepdims=True)
            out_ref[:, columns(h)] = jnp.where(keep_row, mixed_ref[h] / total, 0.0).astype(out_ref.dtype)

    @pl.when(start >= live)
    def _():
        out_ref[...] = jnp.zeros_like(out_ref)


def attention(qheads, first, here, pages, prefix, live, queries, keys, values, parts, carry):
    most = MAXP // 4 + 1
    width = qheads * HD
    if carry is None:
        carry = jnp.zeros((16, 128), jnp.bfloat16)
        aliases = {}
    else:
        aliases = {7 + len(parts): 0}

    def at(half, *_):
        return (first * 2 + half, 0)

    return pl.pallas_call(
        functools.partial(attend_kernel, qheads, (len(parts) + 2) // 4),
        grid_spec=pltpu.PrefetchScalarGridSpec(
            num_scalar_prefetch=4,
            grid=(2,),
            in_specs=[
                pl.BlockSpec((SPAN, width), at),
                pl.BlockSpec((SUF, HD), lambda *_: (first, 0)),
                pl.BlockSpec((SUF, HD), lambda *_: (first, 0)),
            ]
            + [IN_HBM] * len(parts)
            + [ANYWHERE],
            out_specs=pl.BlockSpec((SPAN, width), at),
            scratch_shapes=[
                pltpu.VMEM((MAXP + 2, 2, PAGE, HD), jnp.bfloat16),
                pltpu.VMEM((most, qheads, SPAN, 4 * PAGE), jnp.float32),
                pltpu.VMEM((qheads, SPAN, HD), jnp.float32),
                pltpu.VMEM((qheads, SPAN, HD), jnp.float32),
                pltpu.VMEM((qheads, SPAN, HD), jnp.float32),
                pltpu.SemaphoreType.DMA,
            ],
        ),
        out_shape=jax.ShapeDtypeStruct(queries.shape, jnp.bfloat16),
        input_output_aliases=aliases,
        compiler_params=pltpu.CompilerParams(vmem_limit_bytes=VMEM),
        cost_estimate=pl.CostEstimate(
            flops=qheads * SUF * (MAXP * PAGE + SUF) * HD * 4,
            bytes_accessed=SUF * qheads * HD * 4 + MAXP * PAGE * HD * 4,
            transcendentals=qheads * SUF * (MAXP * PAGE + SUF),
        ),
        name="attention",
    )(here, pages, prefix, live, queries, keys, values, *parts, carry)


def after(value, *others):
    return lax.optimization_barrier((value,) + others)[0]


def body(
    mixer_input,
    step_raw,
    decay_rate,
    skip_gain,
    state_proj,
    queries,
    suffix_kv,
    state_pool,
    page_pool,
    norm_gain,
    hit_owner,
    hit_slot,
    page_owner,
    page_slot,
    prefix_len,
    suffix_len,
):
    owners = lax.axis_size("owner")
    owner = lax.axis_index("owner").astype(jnp.int32)
    column = lax.axis_index("tensor")
    rows = mixer_input.shape[0]
    count = rows // SUF
    heads = decay_rate.shape[0]
    width = heads * MHDIM
    qheads = queries.shape[1] // HD
    per_group = SSM_HEAD_TOTAL // GROUPS
    group = column * heads // per_group
    kv_index = column * qheads // (QHEADS // KVHEADS)
    whole_group = heads == per_group
    chips = owners // 2
    per_chip = 2 * SLOTS_DEV
    states = owners * SLOTS_DEV
    here = owner.reshape(1)
    first = (owner * count).reshape(1)
    swap = [(o, o ^ 1) for o in range(owners)]

    def line(hop):
        up = [(o, o + 2) for o in range(0, owners - 2, 2) if o // 2 >= hop - 1]
        return up + [(o, o - 2) for o in range(3, owners, 2) if o // 2 <= chips - hop]

    def send(item, step):
        up = [(o, o + 2) for o in range(0, owners - 2, 2) if step >= HOP_STEPS * (o // 2)]
        down = [(o, o - 2) for o in range(3, owners, 2) if step >= HOP_STEPS * (chips - 1 - o // 2)]
        return lax.ppermute(item, "owner", up + down)

    def head_of(array, index, axis):
        return lax.dynamic_index_in_dim(array, index, axis, keepdims=False)

    pool = state_pool.reshape(SLOTS_DEV, width, STATE)
    near = lax.ppermute(pool, "owner", swap)
    own_pages = jnp.transpose(head_of(page_pool, kv_index, 3), (0, 2, 1, 3))
    near_pages = lax.ppermute(own_pages, "owner", swap)

    state_ids = (hit_owner[:, 0] * SLOTS_DEV + hit_slot).astype(jnp.int32)
    table, cap = route(after(state_ids, near_pages), owner, chips, per_chip, 2 * count)

    spread_np = np.zeros((128, width), np.float32)
    for h in range(heads):
        for k in range(3):
            spread_np[k * heads + h, h * MHDIM : (h + 1) * MHDIM] = 1.0
    spread = jnp.asarray(spread_np, jnp.bfloat16)
    split_np = np.zeros((2 * SPAN, 2 * SPAN), np.float32)
    for i in range(SPAN):
        split_np[i, 2 * i] = 1.0
        split_np[SPAN + i, 2 * i + 1] = 1.0
    split = jnp.asarray(split_np, jnp.bfloat16)
    skip = jnp.repeat(skip_gain, MHDIM)[None, :]
    decay = jnp.broadcast_to(decay_rate[:, None], (heads, SPAN))
    step_row = step_raw.T
    page_ids = (page_owner[:, :, 0] * PAGES_DEV + page_slot).astype(jnp.int32).reshape(-1)
    made = {}

    def shape_inputs(tie):
        maps = head_of(after(state_proj, tie), group, 2)
        made["b"], made["c"] = maps[:, 0], maps[:, 1]
        suffix = head_of(after(suffix_kv, tie), kv_index, 2)
        made["k"], made["v"] = suffix[:, 0], suffix[:, 1]
        return made["b"], made["k"]

    def pre_part(r):
        def run(tie):
            made["pre"] = mamba_pre(
                heads,
                r,
                2,
                suffix_len,
                after(first, tie),
                mixer_input,
                made["b"],
                made["c"],
                step_row,
                decay,
                skip,
                spread,
                split,
                made.get("pre"),
            )
            return (made["pre"][2],)

        return run

    def attention_part(r):
        def run(tie):
            place = jnp.concatenate([first + r, here])
            made["attn"] = attention(
                qheads,
                r,
                after(place, tie),
                page_ids,
                prefix_len,
                suffix_len,
                queries,
                made["k"],
                made["v"],
                made["parts"],
                made.get("attn"),
            )
            return (made["attn"],)

        return run

    def step_at(step):
        return jnp.full((1,), step, jnp.int32)

    beside = [shape_inputs] + [pre_part(r) for r in range(0, count, 2)]
    ours, theirs, came = [], [], []
    pieces = [own_pages, near_pages]
    for hop in range(1, chips):
        got = [lax.ppermute(piece, "owner", line(hop)) for piece in pieces]
        tie = pieces[1]
        if hop == 1:
            done = (table, near)
        else:
            step = HOP_STEPS * (hop - 2)
            items = take(states, HOP_STEPS, here, table, step_at(step), pool, near, came)
            items = [after(item, piece) for item, piece in zip(items, pieces)]
            came += [send(item, step + k) for k, item in enumerate(items)]
            tie = items[0]
            done = ()
        if beside:
            done += beside.pop(0)(tie)
        pieces = [after(piece, *done) for piece in got]
        ours += pieces
        theirs += [lax.ppermute(piece, "owner", swap) for piece in pieces]
    made["parts"] = [own_pages, near_pages] + ours + theirs

    beside += [attention_part(r) for r in range(count)]
    started = HOP_STEPS * (chips - 2)
    fixed = started + FREE_STEPS
    items = take(states, LAG, after(here, pieces[1]), table, step_at(started), pool, near, came)
    flying = [send(item, started + k) for k, item in enumerate(items)]
    tie = items[-1]
    for step in range(started + LAG, fixed):
        done = ()
        if (step - started) % 2 == 0 and beside:
            done = beside.pop(0)(tie)
        came.append(after(flying.pop(0), *done))
        (item,) = take(states, 1, here, table, step_at(step), pool, near, came)
        flying.append(send(item, step))
        tie = item
    done = ()
    while beside:
        done = beside.pop(0)(tie)
        tie = done[0]
    came.append(after(flying[0], *done))
    came.append(flying[1])

    def more(step, room):
        (item,) = take(states, 1, here, table, step.reshape(1), pool, near, came, room)
        return keep(fixed, step.reshape(1), send(item, fixed), room)

    room = blank(here, (cap - fixed,) + pool.shape[1:], pool.dtype)
    room = lax.fori_loop(fixed, table[2 * cap], more, room)

    picked = pick(states, cap, count, table, came, room)
    other = lax.ppermute(picked, "owner", swap)
    result = None
    for place in (after(here, picked), here):
        result = mamba_post(
            heads,
            whole_group,
            cap,
            states,
            place,
            table,
            suffix_len,
            pool,
            near,
            came,
            room,
            other,
            made["c"],
            *made["pre"],
            spread,
            norm_gain[None, :],
            result,
        )
    if whole_group:
        return (result[0], made["attn"])
    gated, partial_sum = result
    partial_sum = partial_sum[:, 0]
    spread_sum = jnp.where(jnp.arange(GROUPS)[:, None] == group, partial_sum[None, :], 0.0)
    totals = lax.psum(spread_sum, "tensor")
    square = lax.dynamic_index_in_dim(totals, group, 0, keepdims=False) / (per_group * MHDIM)
    my_suffix = lax.dynamic_slice_in_dim(suffix_len, first[0], count, 0)
    active = (jnp.arange(SUF)[None, :] < my_suffix[:, None]).reshape(-1)
    scaled = gated * lax.rsqrt(square + EPSILON)[:, None] * norm_gain[None, :]
    return (jnp.where(active[:, None], scaled, 0.0).astype(jnp.bfloat16), made["attn"])


def solution(mesh):
    return jax.shard_map(
        body,
        mesh=mesh,
        in_specs=(
            P("owner", None, "tensor"),
            P("owner", "tensor"),
            P("tensor"),
            P("tensor"),
            P("owner", None, None, None),
            P("owner", "tensor"),
            P("owner", None, None, None),
            P("owner", "tensor"),
            P("owner", None, None, None, None),
            P("tensor"),
            P(),
            P(),
            P(),
            P(),
            P(),
            P(),
        ),
        out_specs=(P("owner", "tensor"), P("owner", "tensor")),
        check_vma=False,
    )
```

profile of v0, /device:TPU:0, one launch (start us, length us, event | category | flops | bytes accessed | tf_op | source)
XLA Modules:
  0.0 207.2 jit_solution(8144562956064741260)
XLA Ops:
  0.7 0.5 collective-permute-start.2
  1.2 4.7 %constant_dynamic-slice_fusion.2 = bf16[16,128,2,1,128]{4,3,2,1,0:T(2,128)(2,1)S(1)} fusion(bf16[16,128,2,4,128]{4,3,2,1,0:T(4,128)(2,1)} %param.28, s32[]{:T(128)S(6)} %select_n.19), kind=kLoop, calls=%fused_computation.10 | loop fusion | bytes 2097156 | tf_op jit(solution)/shard_map/jit(dynamic_index_in_dim)/dynamic_slice | solution.py:904
  5.9 0.3 copy.41
  6.2 0.2 collective-permute-start.1
  6.4 5.8 %collective-permute-start.3 = (bf16[16,2,128,128]{3,2,1,0:T(8,128)(2,1)S(1)}, bf16[16,2,128,128]{3,2,1,0:T(8,128)(2,1)}, u32[]{:S(2)}, u32[]{:S(2)}) collective-permute-start(bf16[16,2,128,128]{3,2,1,0:T(8,128)(2,1)S(1)} %bitcast.34), channel_id=1, source_target_pairs={{0,8},{8,16},{16,24},{12,4},{20,12},{28,20},{1,9},{9,17},{17,25},{... | collective-permute-start | bytes 3145736 | tf_op jit(solution)/shard_map/ppermute | solution.py:986
  12.2 0.5 bitcast_add_fusion.1.ids_ref
  12.7 4.3 %constant_dynamic-slice_fusion.1 = bf16[1024,2,1,256]{3,2,1,0:T(2,128)(2,1)S(1)} fusion(bf16[1024,2,4,256]{3,2,1,0:T(4,128)(2,1)} %param.24, s32[]{:T(128)S(6)} %select_n.21), kind=kLoop, calls=%fused_computation.9 | loop fusion | bytes 2097156 | tf_op jit(solution)/shard_map/jit(dynamic_index_in_dim)/dynamic_slice | solution.py:904
  17.0 1.1 copy.40
  18.2 1.1 constant_dynamic-slice_fusion
  19.3 0.1 copy.42
  19.4 4.3 %route_states.1.table_ref = s32[132]{0:T(256)S(1)} custom-call(s32[32]{0:T(128)} %bitcast_add_fusion.1.ids_ref, s32[1]{0:T(128)} %bitcast.1.here_ref), custom_call_target="tpu_custom_call" | custom-call | tf_op jit(solution)/shard_map/route_states/pallas_call | solution.py:165
  23.6 2.6 %collective-permute-start.5 = (bf16[16,2,128,128]{3,2,1,0:T(8,128)(2,1)}, bf16[16,2,128,128]{3,2,1,0:T(8,128)(2,1)S(1)}, u32[]{:S(2)}, u32[]{:S(2)}) collective-permute-start(bf16[16,2,128,128]{3,2,1,0:T(8,128)(2,1)} %collective-permute-done.1.rest_1_), channel_id=1, source_target_pairs={{0,8},{8,16},{16,24},{12,4},{20,12},{28,20},{1,9},{9,17},{17,25},{... | collective-permute-start | bytes 3145736 | tf_op jit(solution)/shard_map/ppermute | solution.py:986
  26.3 0.7 slice_bitcast_fusion.2
  27.0 2.2 %slice_bitcast_fusion = (bf16[1024,256]{1,0:T(8,128)(2,1)}, bf16[1024,256]{1,0:T(8,128)(2,1)}) fusion(bf16[1024,2,256]{2,0,1:T(8,128)(2,1)} %bitcast.53), kind=kLoop, calls=%fused_computation.2 | loop fusion | bytes 2097152 | tf_op jit(solution)/shard_map/squeeze | solution.py:932
  29.3 0.7 collective-permute-start.7
  30.1 0.1 broadcast_in_dim_reshape.3.skip_ref
  30.2 2.9 %take_states.9 = (bf16[2048,256]{1,0:T(8,128)(2,1)}, bf16[2048,256]{1,0:T(8,128)(2,1)}) custom-call(s32[1]{0:T(128)} %bitcast.1.here_ref, s32[132]{0:T(256)S(1)} %route_states.1.table_ref, s32[1]{0:T(128)} %constant.70.clone.1.step_ref, bf16[4,2048,256]{2,1,0:T(8,128)(2,1)} %bitcast.44, bf16[4,2048,256]{2,1,0:T(8,128)(2,1)} %collective-permute-done.2.near_ref.rest_1_), custom_call_target="tpu_custom_call" | custom-call | tf_op jit(solution)/shard_map/take_states/pallas_call | solution.py:255
  33.1 4.3 %collective-permute-start.4 = (bf16[2048,256]{1,0:T(8,128)(2,1)}, bf16[2048,256]{1,0:T(8,128)(2,1)}, u32[]{:S(2)}, u32[]{:S(2)}) collective-permute-start(bf16[2048,256]{1,0:T(8,128)(2,1)} %get-tuple-element.137), channel_id=1, source_target_pairs={{0,8},{28,20},{1,9},{29,21},{2,10},{30,22},{3,11},{31,23}} | collective-permute-start | bytes 3145736 | tf_op jit(solution)/shard_map/ppermute | solution.py:901
  37.5 1.4 collective-permute-done.5.rest_3_
  38.8 1.6 collective-permute-start.9
  40.5 8.1 %collective-permute-start.6 = (bf16[2048,256]{1,0:T(8,128)(2,1)}, bf16[2048,256]{1,0:T(8,128)(2,1)}, u32[]{:S(2)}, u32[]{:S(2)}) collective-permute-start(bf16[2048,256]{1,0:T(8,128)(2,1)} %get-tuple-element.140), channel_id=1, source_target_pairs={{0,8},{28,20},{1,9},{29,21},{2,10},{30,22},{3,11},{31,23}} | collective-permute-start | bytes 3145736 | tf_op jit(solution)/shard_map/ppermute | solution.py:901
  48.7 11.0 %mamba_pre.2 = (f32[1024,2048]{1,0:T(8,128)}, bf16[1024,2048]{1,0:T(8,128)(2,1)}, bf16[1024,128]{1,0:T(8,128)(2,1)S(1)}) custom-call(s32[32]{0:T(128)S(1)} %copy-done.18, s32[1]{0:T(128)} %bitcast.11.first_ref, bf16[1024,2,2048]{2,1,0:T(2,128)(2,1)} %mix_ref.3, bf16[1024,256]{1,0:T(8,128)(2,1)S(1)} %copy-done.12, bf16[1024,256]{1,0:T(8,128)(2,1)S(1)} %copy-done.3, ...), custom_call_target="tpu_custom_call" | custom-call | flops 5368709120 | bytes 10485760 | tf_op jit(solution)/shard_map/mamba_pre/pallas_call | solution.py:467
  59.7 1.7 collective-permute-start.13
  61.4 1.6 collective-permute-start.11
  63.0 2.9 %take_states.10 = (bf16[2048,256]{1,0:T(8,128)(2,1)}, bf16[2048,256]{1,0:T(8,128)(2,1)}) custom-call(s32[1]{0:T(128)} %bitcast.1.here_ref, s32[132]{0:T(256)S(1)} %route_states.1.table_ref, s32[1]{0:T(128)} %constant.74.clone.1.step_ref, bf16[4,2048,256]{2,1,0:T(8,128)(2,1)} %bitcast.45, bf16[4,2048,256]{2,1,0:T(8,128)(2,1)} %collective-permute-done.2.near_ref.rest_1_, ...), custom_call_target="tpu_custom_call" | custom-call | tf_op jit(solution)/shard_map/take_states/pallas_call | solution.py:255
  65.9 4.4 %collective-permute-start.10 = (bf16[2048,256]{1,0:T(8,128)(2,1)}, bf16[2048,256]{1,0:T(8,128)(2,1)}, u32[]{:S(2)}, u32[]{:S(2)}) collective-permute-start(bf16[2048,256]{1,0:T(8,128)(2,1)} %get-tuple-element.148), channel_id=1, source_target_pairs={{0,8},{8,16},{20,12},{28,20},{1,9},{9,17},{21,13},{29,21},{2,10},{... | collective-permute-start | bytes 3145736 | tf_op jit(solution)/shard_map/ppermute | solution.py:901
  70.3 4.3 %collective-permute-start.8 = (bf16[2048,256]{1,0:T(8,128)(2,1)}, bf16[2048,256]{1,0:T(8,128)(2,1)}, u32[]{:S(2)}, u32[]{:S(2)}) collective-permute-start(bf16[2048,256]{1,0:T(8,128)(2,1)} %get-tuple-element.145), channel_id=1, source_target_pairs={{0,8},{8,16},{20,12},{28,20},{1,9},{9,17},{21,13},{29,21},{2,10},{... | collective-permute-start | bytes 3145736 | tf_op jit(solution)/shard_map/ppermute | solution.py:901
  74.6 9.5 %mamba_pre.3 = (f32[1024,2048]{1,0:T(8,128)}, bf16[1024,2048]{1,0:T(8,128)(2,1)}, bf16[1024,128]{1,0:T(8,128)(2,1)S(1)}) custom-call(s32[32]{0:T(128)S(1)} %copy-done.18, s32[1]{0:T(128)S(6)} %add.36.first_ref, bf16[1024,2,2048]{2,1,0:T(2,128)(2,1)} %mix_ref.3, ...), custom_call_target="tpu_custom_call", output_to_operand_aliasing={{0}: (10, {}), {1}: (11, {}), {2}: (12, {})} | custom-call | flops 5368709120 | bytes 10485760 | tf_op jit(solution)/shard_map/mamba_pre/pallas_call | solution.py:467
  84.1 2.1 collective-permute-start.17
  86.2 0.1 collective-permute-start.16
  86.3 0.4 collective-permute-start.18
  86.7 6.4 %collective-permute-done.8.rest_2_.rest_4_ = bf16[2048,256]{1,0:T(8,128)(2,1)} collective-permute-done((bf16[2048,256]{1,0:T(8,128)(2,1)}, bf16[2048,256]{1,0:T(8,128)(2,1)}, u32[]{:S(2)}, u32[]{:S(2)}) %collective-permute-start.8) | collective-permute-done | bytes 1048608 | tf_op jit(solution)/shard_map/ppermute | solution.py:901
  93.1 2.5 %take_states.11 = (bf16[2048,256]{1,0:T(8,128)(2,1)}, bf16[2048,256]{1,0:T(8,128)(2,1)}) custom-call(s32[1]{0:T(128)} %bitcast.1.here_ref, s32[132]{0:T(256)S(1)} %route_states.1.table_ref, s32[1]{0:T(128)} %constant.76.clone.1.step_ref, bf16[4,2048,256]{2,1,0:T(8,128)(2,1)} %bitcast.46, bf16[4,2048,256]{2,1,0:T(8,128)(2,1)} %collective-permute-done.2.near_ref.rest_1_, ...), custom_call_target="tpu_custom_call" | custom-call | tf_op jit(solution)/shard_map/take_states/pallas_call | solution.py:255
  95.7 5.8 %collective-permute-start.12 = (bf16[2048,256]{1,0:T(8,128)(2,1)}, bf16[2048,256]{1,0:T(8,128)(2,1)}, u32[]{:S(2)}, u32[]{:S(2)}) collective-permute-start(bf16[2048,256]{1,0:T(8,128)(2,1)} %get-tuple-element.155), channel_id=1, source_target_pairs={{0,8},{8,16},{16,24},{12,4},{20,12},{28,20},{1,9},{9,17},{17,25},{... | collective-permute-start | bytes 3145736 | tf_op jit(solution)/shard_map/ppermute | solution.py:901
  101.4 0.1 copy.36
  101.5 0.1 reshape.29.pages_ref
  101.7 3.5 %collective-permute-start.20 = (bf16[2048,256]{1,0:T(8,128)(2,1)}, bf16[2048,256]{1,0:T(8,128)(2,1)S(1)}, u32[]{:S(2)}, u32[]{:S(2)}) collective-permute-start(bf16[2048,256]{1,0:T(8,128)(2,1)} %get-tuple-element.156), channel_id=1, source_target_pairs={{0,8},{8,16},{16,24},{12,4},{20,12},{28,20},{1,9},{9,17},{17,25},{... | collective-permute-start | bytes 3145736 | tf_op jit(solution)/shard_map/ppermute | solution.py:901
  105.2 0.9 copy-done.5
  106.1 13.2 %attention.4.rest_14_ = bf16[1024,1024]{1,0:T(8,128)(2,1)} custom-call(s32[2]{0:T(128)S(1)} %pad_add_fusion.first_ref, s32[512]{0:T(512)S(1)} %reshape.29.pages_ref, s32[32]{0:T(128)S(1)} %copy-done.19, s32[32]{0:T(128)S(1)} %copy-done.18, bf16[1024,1024]{1,0:T(8,128)(2,1)} %q_ref.7, bf16[1024,128]{1,0:T(8,128)(2,1)S(1)} %copy-done.5, ...), custom_call_target="tpu_custom_call" | custom-call | flops 2415919104 | bytes 2097152 | tf_op jit(solution)/shard_map/attention/pallas_call | solution.py:819
  119.3 0.6 take_states.12
  120.0 1.4 collective-permute-start.21
  121.4 2.9 %collective-permute-done.20.rest_5_.rest_7_ = bf16[2048,256]{1,0:T(8,128)(2,1)S(1)} collective-permute-done((bf16[2048,256]{1,0:T(8,128)(2,1)}, bf16[2048,256]{1,0:T(8,128)(2,1)S(1)}, u32[]{:S(2)}, u32[]{:S(2)}) %collective-permute-start.20) | collective-permute-done | bytes 1048608 | tf_op jit(solution)/shard_map/ppermute | solution.py:901
  124.3 0.6 take_states.13
  124.9 7.3 %collective-permute-start.22 = (bf16[2048,256]{1,0:T(8,128)(2,1)}, bf16[2048,256]{1,0:T(8,128)(2,1)}, u32[]{:S(2)}, u32[]{:S(2)}) collective-permute-start(bf16[2048,256]{1,0:T(8,128)(2,1)} %take_states.13), channel_id=1, source_target_pairs={{0,8},{8,16},{16,24},{12,4},{20,12},{28,20},{1,9},{9,17},{17,25},{... | collective-permute-start | bytes 3145736 | tf_op jit(solution)/shard_map/ppermute | solution.py:901
  132.2 5.9 %attention.5.rest_14_ = bf16[1024,1024]{1,0:T(8,128)(2,1)} custom-call(s32[2]{0:T(128)S(1)} %pad_add_fusion.1.first_ref, s32[512]{0:T(512)S(1)} %reshape.29.pages_ref, s32[32]{0:T(128)S(1)} %copy-done.19, s32[32]{0:T(128)S(1)} %copy-done.18, bf16[1024,1024]{1,0:T(8,128)(2,1)} %q_ref.7, ...), custom_call_target="tpu_custom_call", output_to_operand_aliasing={{}: (21, {})} | custom-call | flops 2415919104 | bytes 2097152 | tf_op jit(solution)/shard_map/attention/pallas_call | solution.py:819
  138.2 0.6 take_states.14
  138.8 2.7 %collective-permute-start.23 = (bf16[2048,256]{1,0:T(8,128)(2,1)}, bf16[2048,256]{1,0:T(8,128)(2,1)}, u32[]{:S(2)}, u32[]{:S(2)}) collective-permute-start(bf16[2048,256]{1,0:T(8,128)(2,1)} %take_states.14), channel_id=1, source_target_pairs={{0,8},{8,16},{16,24},{12,4},{20,12},{28,20},{1,9},{9,17},{17,25},{... | collective-permute-start | bytes 3145736 | tf_op jit(solution)/shard_map/ppermute | solution.py:901
  141.6 5.2 %collective-permute-done.22.rest_7_.rest_9_ = bf16[2048,256]{1,0:T(8,128)(2,1)} collective-permute-done((bf16[2048,256]{1,0:T(8,128)(2,1)}, bf16[2048,256]{1,0:T(8,128)(2,1)}, u32[]{:S(2)}, u32[]{:S(2)}) %collective-permute-start.22) | collective-permute-done | bytes 1048608 | tf_op jit(solution)/shard_map/ppermute | solution.py:901
  146.8 0.6 take_states.15
  147.4 5.4 %collective-permute-start.24 = (bf16[2048,256]{1,0:T(8,128)(2,1)}, bf16[2048,256]{1,0:T(8,128)(2,1)}, u32[]{:S(2)}, u32[]{:S(2)}) collective-permute-start(bf16[2048,256]{1,0:T(8,128)(2,1)} %take_states.15), channel_id=1, source_target_pairs={{0,8},{8,16},{16,24},{12,4},{20,12},{28,20},{1,9},{9,17},{17,25},{... | collective-permute-start | bytes 3145736 | tf_op jit(solution)/shard_map/ppermute | solution.py:901
  152.8 4.6 %attention.6.rest_14_ = bf16[1024,1024]{1,0:T(8,128)(2,1)} custom-call(s32[2]{0:T(128)S(1)} %pad_add_fusion.2.first_ref, s32[512]{0:T(512)S(1)} %reshape.29.pages_ref, s32[32]{0:T(128)S(1)} %copy-done.19, s32[32]{0:T(128)S(1)} %copy-done.18, bf16[1024,1024]{1,0:T(8,128)(2,1)} %q_ref.7, ...), custom_call_target="tpu_custom_call", output_to_operand_aliasing={{}: (21, {})} | custom-call | flops 2415919104 | bytes 2097152 | tf_op jit(solution)/shard_map/attention/pallas_call | solution.py:819
  157.4 0.6 collective-permute-done.23.rest_8_.rest_10_
  158.0 0.6 take_states.16
  158.7 5.4 %collective-permute-start.25 = (bf16[2048,256]{1,0:T(8,128)(2,1)}, bf16[2048,256]{1,0:T(8,128)(2,1)}, u32[]{:S(2)}, u32[]{:S(2)}) collective-permute-start(bf16[2048,256]{1,0:T(8,128)(2,1)} %take_states.16), channel_id=1, source_target_pairs={{0,8},{8,16},{16,24},{12,4},{20,12},{28,20},{1,9},{9,17},{17,25},{... | collective-permute-start | bytes 3145736 | tf_op jit(solution)/shard_map/ppermute | solution.py:901
  164.2 0.6 slice.19
  164.8 0.9 copy-done.7
  165.7 5.6 %attention.7 = bf16[1024,1024]{1,0:T(8,128)(2,1)} custom-call(s32[2]{0:T(128)S(1)} %pad_add_fusion.3.first_ref, s32[512]{0:T(512)S(1)} %reshape.29.pages_ref, s32[32]{0:T(128)S(1)} %copy-done.19, s32[32]{0:T(128)S(1)} %copy-done.18, bf16[1024,1024]{1,0:T(8,128)(2,1)} %q_ref.7, bf16[1024,128]{1,0:T(8,128)(2,1)S(1)} %copy-done.7, ...), custom_call_target="tpu_custom_call", output_to_operand_aliasing={{}: (21, {})} | custom-call | flops 2415919104 | bytes 2097152 | tf_op jit(solution)/shard_map/attention/pallas_call | solution.py:819
  171.4 9.1 %collective-permute-done.25.rest_10_.rest_12_ = bf16[2048,256]{1,0:T(8,128)(2,1)} collective-permute-done((bf16[2048,256]{1,0:T(8,128)(2,1)}, bf16[2048,256]{1,0:T(8,128)(2,1)}, u32[]{:S(2)}, u32[]{:S(2)}) %collective-permute-start.25) | collective-permute-done | bytes 1048608 | tf_op jit(solution)/shard_map/ppermute | solution.py:901
  180.5 0.6 while.10
  181.1 0.8 pick_states.1
  181.9 6.7 %collective-permute-start.26 = (bf16[4,2048,256]{2,1,0:T(8,128)(2,1)}, bf16[4,2048,256]{2,1,0:T(8,128)(2,1)S(1)}, u32[]{:S(2)}, u32[]{:S(2)}) collective-permute-start(bf16[4,2048,256]{2,1,0:T(8,128)(2,1)} %pick_states.1), channel_id=1, source_target_pairs={{0,4},{4,0},{8,12},{12,8},{16,20},{20,16},{24,28},{28,24},{1,5},{5... | collective-permute-start | bytes 12582920 | tf_op jit(solution)/shard_map/ppermute | solution.py:1033
  188.7 2.6 %mamba_post.2.rest_21_ = bf16[1024,2048]{1,0:T(8,128)(2,1)} custom-call(s32[1]{0:T(128)} %bitcast.1.here_ref, s32[132]{0:T(256)S(1)} %get-tuple-element.400, s32[32]{0:T(128)S(1)} %copy-done.18, bf16[4,2048,256]{2,1,0:T(8,128)(2,1)} %get-tuple-element.387, bf16[4,2048,256]{2,1,0:T(8,128)(2,1)} %collective-permute-done.2.near_ref.rest_1_, ...), custom_call_target="tpu_custom_call" | custom-call | flops 1073741824 | bytes 12582912 | tf_op jit(solution)/shard_map/mamba_post/pallas_call | solution.py:632
  191.2 4.4 %collective-permute-done.26.rest_14_ = bf16[4,2048,256]{2,1,0:T(8,128)(2,1)S(1)} collective-permute-done((bf16[4,2048,256]{2,1,0:T(8,128)(2,1)}, bf16[4,2048,256]{2,1,0:T(8,128)(2,1)S(1)}, u32[]{:S(2)}, u32[]{:S(2)}) %collective-permute-start.26) | collective-permute-done | bytes 4194336 | tf_op jit(solution)/shard_map/ppermute | solution.py:1033
  195.6 11.4 %mamba_post.3 = bf16[1024,2048]{1,0:T(8,128)(2,1)} custom-call(s32[1]{0:T(128)} %bitcast.1.here_ref, s32[132]{0:T(256)S(1)} %get-tuple-element.400, s32[32]{0:T(128)S(1)} %copy-done.18, bf16[4,2048,256]{2,1,0:T(8,128)(2,1)S(1)} %copy-done.20, bf16[4,2048,256]{2,1,0:T(8,128)(2,1)} %collective-permute-done.2.near_ref.rest_1_, ...), custom_call_target="tpu_custom_call", output_to_operand_aliasing={{}: (24, {})} | custom-call | flops 1073741824 | bytes 12582912 | tf_op jit(solution)/shard_map/mamba_post/pallas_call | solution.py:632
  (90 shorter events, 0.7 us)
Async XLA Ops:
  0.6 17.5 %copy-start = (bf16[1024,2,4,128]{3,2,1,0:T(4,128)(2,1)S(1)}, bf16[1024,2,4,128]{3,2,1,0:T(4,128)(2,1)}, u32[]{:S(2)}) copy-start(bf16[1024,2,4,128]{3,2,1,0:T(4,128)(2,1)} %param.26) | copy-start | bytes 6291460
  0.6 11.5 %copy-start.30 = (s32[32,1]{0,1:T(1,128)S(1)}, s32[32,1]{0,1:T(1,128)}, u32[]{:S(2)}) copy-start(s32[32,1]{0,1:T(1,128)} %param.30) | copy-start | bytes 388
  0.7 11.5 %copy-start.29 = (s32[32]{0:T(128)S(1)}, s32[32]{0:T(128)}, u32[]{:S(2)}) copy-start(s32[32]{0:T(128)} %param.31) | copy-start | bytes 388
  0.7 28.6 %collective-permute-start.2 = (bf16[4,2048,256]{2,1,0:T(8,128)(2,1)}, bf16[4,2048,256]{2,1,0:T(8,128)(2,1)}, u32[]{:S(2)}, u32[]{:S(2)}) collective-permute-start(bf16[4,2048,256]{2,1,0:T(8,128)(2,1)} %bitcast.43), channel_id=1, source_target_pairs={{0,4},{4,0},{8,12},{12,8},{16,20},{20,16},{24,28},{28,24},{1,5},{5... | collective-permute-start | bytes 12582920 | tf_op jit(solution)/shard_map/ppermute | solution.py:907
  6.2 6.5 %collective-permute-start.1 = (bf16[16,2,128,128]{3,2,1,0:T(8,128)(2,1)S(1)}, bf16[16,2,128,128]{3,2,1,0:T(8,128)(2,1)}, u32[]{:S(2)}, u32[]{:S(2)}) collective-permute-start(bf16[16,2,128,128]{3,2,1,0:T(8,128)(2,1)S(1)} %bitcast.33), channel_id=1, source_target_pairs={{0,4},{4,0},{8,12},{12,8},{16,20},{20,16},{24,28},{28,24},{1,5},{5... | collective-permute-start | bytes 3145736 | tf_op jit(solution)/shard_map/ppermute | solution.py:909
  6.4 22.9 %collective-permute-start.3 = (bf16[16,2,128,128]{3,2,1,0:T(8,128)(2,1)S(1)}, bf16[16,2,128,128]{3,2,1,0:T(8,128)(2,1)}, u32[]{:S(2)}, u32[]{:S(2)}) collective-permute-start(bf16[16,2,128,128]{3,2,1,0:T(8,128)(2,1)S(1)} %bitcast.34), channel_id=1, source_target_pairs={{0,8},{8,16},{16,24},{12,4},{20,12},{28,20},{1,9},{9,17},{17,25},{... | collective-permute-start | bytes 3145736 | tf_op jit(solution)/shard_map/ppermute | solution.py:986
  18.2 11.8 %copy-start.27 = (f32[32]{0:T(128)S(1)}, f32[32]{0:T(128)}, u32[]{:S(2)}) copy-start(f32[32]{0:T(128)} %param.23) | copy-start | bytes 388
  23.6 15.2 %collective-permute-start.5 = (bf16[16,2,128,128]{3,2,1,0:T(8,128)(2,1)}, bf16[16,2,128,128]{3,2,1,0:T(8,128)(2,1)S(1)}, u32[]{:S(2)}, u32[]{:S(2)}) collective-permute-start(bf16[16,2,128,128]{3,2,1,0:T(8,128)(2,1)} %collective-permute-done.1.rest_1_), channel_id=1, source_target_pairs={{0,8},{8,16},{16,24},{12,4},{20,12},{28,20},{1,9},{9,17},{17,25},{... | collective-permute-start | bytes 3145736 | tf_op jit(solution)/shard_map/ppermute | solution.py:986
  29.3 30.4 %collective-permute-start.7 = (bf16[16,2,128,128]{3,2,1,0:T(8,128)(2,1)}, bf16[16,2,128,128]{3,2,1,0:T(8,128)(2,1)S(1)}, u32[]{:S(2)}, u32[]{:S(2)}) collective-permute-start(bf16[16,2,128,128]{3,2,1,0:T(8,128)(2,1)} %collective-permute-done.3.rest_2_), channel_id=1, source_target_pairs={{8,16},{16,24},{12,4},{20,12},{9,17},{17,25},{13,5},{21,13},{10,18... | collective-permute-start | bytes 3145736 | tf_op jit(solution)/shard_map/ppermute | solution.py:986
  30.2 18.4 %copy-start.28 = (f32[32]{0:T(128)S(1)}, f32[32]{0:T(128)}, u32[]{:S(2)}) copy-start(f32[32]{0:T(128)} %param.22) | copy-start | bytes 388
  30.2 18.5 %copy-start.3 = (bf16[1024,256]{1,0:T(8,128)(2,1)S(1)}, bf16[1024,256]{1,0:T(8,128)(2,1)}, u32[]{:S(2)}) copy-start(bf16[1024,256]{1,0:T(8,128)(2,1)} %get-tuple-element.206.c_ref.rest_15_) | copy-start | bytes 1572868
  30.2 18.5 %copy-start.8 = (bf16[128,2048]{1,0:T(8,128)(2,1)S(1)}, bf16[128,2048]{1,0:T(8,128)(2,1)}, u32[]{:S(2)}) copy-start(bf16[128,2048]{1,0:T(8,128)(2,1)} %constant.87.clone.spread_ref.rest_19_) | copy-start | bytes 1572868
  30.2 18.5 %copy-start.12 = (bf16[1024,256]{1,0:T(8,128)(2,1)S(1)}, bf16[1024,256]{1,0:T(8,128)(2,1)}, u32[]{:S(2)}) copy-start(bf16[1024,256]{1,0:T(8,128)(2,1)} %get-tuple-element.207.b_ref) | copy-start | bytes 1572868
  30.2 18.4 %copy-start.13 = (f32[1024,32]{0,1:T(8,128)S(1)}, f32[1024,32]{0,1:T(8,128)}, u32[]{:S(2)}) copy-start(f32[1024,32]{0,1:T(8,128)} %param.21) | copy-start | bytes 393220
  30.2 18.4 %copy-start.14 = (bf16[256,256]{1,0:T(8,128)(2,1)S(1)}, bf16[256,256]{1,0:T(8,128)(2,1)}, u32[]{:S(2)}) copy-start(bf16[256,256]{1,0:T(8,128)(2,1)} %constant.88.clone.split_ref) | copy-start | bytes 393220
  30.2 18.4 %copy-start.18 = (s32[32]{0:T(128)S(1)}, s32[32]{0:T(128)}, u32[]{:S(2)}) copy-start(s32[32]{0:T(128)} %live_ref.15) | copy-start | bytes 388
  33.1 29.8 %collective-permute-start.4 = (bf16[2048,256]{1,0:T(8,128)(2,1)}, bf16[2048,256]{1,0:T(8,128)(2,1)}, u32[]{:S(2)}, u32[]{:S(2)}) collective-permute-start(bf16[2048,256]{1,0:T(8,128)(2,1)} %get-tuple-element.137), channel_id=1, source_target_pairs={{0,8},{28,20},{1,9},{29,21},{2,10},{30,22},{3,11},{31,23}} | collective-permute-start | bytes 3145736 | tf_op jit(solution)/shard_map/ppermute | solution.py:901
  38.8 22.5 %collective-permute-start.9 = (bf16[16,2,128,128]{3,2,1,0:T(8,128)(2,1)S(1)}, bf16[16,2,128,128]{3,2,1,0:T(8,128)(2,1)}, u32[]{:S(2)}, u32[]{:S(2)}) collective-permute-start(bf16[16,2,128,128]{3,2,1,0:T(8,128)(2,1)S(1)} %collective-permute-done.5.rest_3_), channel_id=1, source_target_pairs={{8,16},{16,24},{12,4},{20,12},{9,17},{17,25},{13,5},{21,13},{10,18... | collective-permute-start | bytes 3145736 | tf_op jit(solution)/shard_map/ppermute | solution.py:986
  40.5 22.5 %collective-permute-start.6 = (bf16[2048,256]{1,0:T(8,128)(2,1)}, bf16[2048,256]{1,0:T(8,128)(2,1)}, u32[]{:S(2)}, u32[]{:S(2)}) collective-permute-start(bf16[2048,256]{1,0:T(8,128)(2,1)} %get-tuple-element.140), channel_id=1, source_target_pairs={{0,8},{28,20},{1,9},{29,21},{2,10},{30,22},{3,11},{31,23}} | collective-permute-start | bytes 3145736 | tf_op jit(solution)/shard_map/ppermute | solution.py:901
  48.7 11.0 %copy-start.15 = (f32[16,128]{1,0:T(8,128)}, f32[16,128]{1,0:T(8,128)S(1)}, u32[]{:S(2)}) copy-start(f32[16,128]{1,0:T(8,128)S(1)} %broadcast_1__pre_in__z_in__e_in_rest_21_.2._pre_in._z_in._e_in.rest_21_) | copy-start | bytes 24580
  59.7 14.9 %collective-permute-start.13 = (bf16[16,2,128,128]{3,2,1,0:T(8,128)(2,1)S(1)}, bf16[16,2,128,128]{3,2,1,0:T(8,128)(2,1)}, u32[]{:S(2)}, u32[]{:S(2)}) collective-permute-start(bf16[16,2,128,128]{3,2,1,0:T(8,128)(2,1)S(1)} %collective-permute-done.7.rest_4_), channel_id=1, source_target_pairs={{16,24},{12,4},{17,25},{13,5},{18,26},{14,6},{19,27},{15,7}} | collective-permute-start | bytes 3145736 | tf_op jit(solution)/shard_map/ppermute | solution.py:986
  61.3 24.9 %collective-permute-start.15 = (bf16[16,2,128,128]{3,2,1,0:T(8,128)(2,1)S(1)}, bf16[16,2,128,128]{3,2,1,0:T(8,128)(2,1)}, u32[]{:S(2)}, u32[]{:S(2)}) collective-permute-start(bf16[16,2,128,128]{3,2,1,0:T(8,128)(2,1)S(1)} %collective-permute-done.5.rest_3_), channel_id=1, source_target_pairs={{0,4},{4,0},{8,12},{12,8},{16,20},{20,16},{24,28},{28,24},{1,5},{5... | collective-permute-start | bytes 3145736 | tf_op jit(solution)/shard_map/ppermute | solution.py:1001
  61.4 22.8 %collective-permute-start.11 = (bf16[16,2,128,128]{3,2,1,0:T(8,128)(2,1)}, bf16[16,2,128,128]{3,2,1,0:T(8,128)(2,1)}, u32[]{:S(2)}, u32[]{:S(2)}) collective-permute-start(bf16[16,2,128,128]{3,2,1,0:T(8,128)(2,1)} %collective-permute-done.9.rest_5_), channel_id=1, source_target_pairs={{16,24},{12,4},{17,25},{13,5},{18,26},{14,6},{19,27},{15,7}} | collective-permute-start | bytes 3145736 | tf_op jit(solution)/shard_map/ppermute | solution.py:986
  65.9 20.4 %collective-permute-start.10 = (bf16[2048,256]{1,0:T(8,128)(2,1)}, bf16[2048,256]{1,0:T(8,128)(2,1)}, u32[]{:S(2)}, u32[]{:S(2)}) collective-permute-start(bf16[2048,256]{1,0:T(8,128)(2,1)} %get-tuple-element.148), channel_id=1, source_target_pairs={{0,8},{8,16},{20,12},{28,20},{1,9},{9,17},{21,13},{29,21},{2,10},{... | collective-permute-start | bytes 3145736 | tf_op jit(solution)/shard_map/ppermute | solution.py:901
  70.3 22.8 %collective-permute-start.8 = (bf16[2048,256]{1,0:T(8,128)(2,1)}, bf16[2048,256]{1,0:T(8,128)(2,1)}, u32[]{:S(2)}, u32[]{:S(2)}) collective-permute-start(bf16[2048,256]{1,0:T(8,128)(2,1)} %get-tuple-element.145), channel_id=1, source_target_pairs={{0,8},{8,16},{20,12},{28,20},{1,9},{9,17},{21,13},{29,21},{2,10},{... | collective-permute-start | bytes 3145736 | tf_op jit(solution)/shard_map/ppermute | solution.py:901
  74.6 21.0 %collective-permute-start.14 = (bf16[16,2,128,128]{3,2,1,0:T(8,128)(2,1)}, bf16[16,2,128,128]{3,2,1,0:T(8,128)(2,1)}, u32[]{:S(2)}, u32[]{:S(2)}) collective-permute-start(bf16[16,2,128,128]{3,2,1,0:T(8,128)(2,1)} %collective-permute-done.3.rest_2_), channel_id=1, source_target_pairs={{0,4},{4,0},{8,12},{12,8},{16,20},{20,16},{24,28},{28,24},{1,5},{5... | collective-permute-start | bytes 3145736 | tf_op jit(solution)/shard_map/ppermute | solution.py:1001
  84.1 11.5 %copy-start.10 = (bf16[1024,128]{1,0:T(8,128)(2,1)}, bf16[1024,128]{1,0:T(8,128)(2,1)S(1)}, u32[]{:S(2)}) copy-start(bf16[1024,128]{1,0:T(8,128)(2,1)S(1)} %get-tuple-element.152.rest_18_) | copy-start | bytes 786436
  84.1 17.3 %copy-start.25 = (s32[32,16]{0,1:T(8,128)S(1)}, s32[32,16]{0,1:T(8,128)}, u32[]{:S(2)}) copy-start(s32[32,16]{0,1:T(8,128)} %param.33) | copy-start | bytes 6148
  84.1 17.3 %copy-start.26 = (s32[32,16,1]{0,2,1:T(1,128)S(1)}, s32[32,16,1]{0,2,1:T(1,128)}, u32[]{:S(2)}) copy-start(s32[32,16,1]{0,2,1:T(1,128)} %param.32) | copy-start | bytes 6148
  84.1 21.1 %copy-start.19 = (s32[32]{0:T(128)S(1)}, s32[32]{0:T(128)}, u32[]{:S(2)}) copy-start(s32[32]{0:T(128)} %prefix_ref.7) | copy-start | bytes 388
  84.1 17.5 %collective-permute-start.17 = (bf16[16,2,128,128]{3,2,1,0:T(8,128)(2,1)}, bf16[16,2,128,128]{3,2,1,0:T(8,128)(2,1)}, u32[]{:S(2)}, u32[]{:S(2)}) collective-permute-start(bf16[16,2,128,128]{3,2,1,0:T(8,128)(2,1)} %collective-permute-done.9.rest_5_), channel_id=1, source_target_pairs={{0,4},{4,0},{8,12},{12,8},{16,20},{20,16},{24,28},{28,24},{1,5},{5... | collective-permute-start | bytes 3145736 | tf_op jit(solution)/shard_map/ppermute | solution.py:1001
  86.2 18.9 %collective-permute-start.16 = (bf16[16,2,128,128]{3,2,1,0:T(8,128)(2,1)S(1)}, bf16[16,2,128,128]{3,2,1,0:T(8,128)(2,1)}, u32[]{:S(2)}, u32[]{:S(2)}) collective-permute-start(bf16[16,2,128,128]{3,2,1,0:T(8,128)(2,1)S(1)} %collective-permute-done.7.rest_4_), channel_id=1, source_target_pairs={{0,4},{4,0},{8,12},{12,8},{16,20},{20,16},{24,28},{28,24},{1,5},{5... | collective-permute-start | bytes 3145736 | tf_op jit(solution)/shard_map/ppermute | solution.py:1001
  86.3 18.9 %collective-permute-start.18 = (bf16[16,2,128,128]{3,2,1,0:T(8,128)(2,1)}, bf16[16,2,128,128]{3,2,1,0:T(8,128)(2,1)}, u32[]{:S(2)}, u32[]{:S(2)}) collective-permute-start(bf16[16,2,128,128]{3,2,1,0:T(8,128)(2,1)} %collective-permute-done.13.rest_6_), channel_id=1, source_target_pairs={{0,4},{4,0},{8,12},{12,8},{16,20},{20,16},{24,28},{28,24},{1,5},{5... | collective-permute-start | bytes 3145736 | tf_op jit(solution)/shard_map/ppermute | solution.py:1001
  93.1 12.1 %collective-permute-start.19 = (bf16[16,2,128,128]{3,2,1,0:T(8,128)(2,1)}, bf16[16,2,128,128]{3,2,1,0:T(8,128)(2,1)}, u32[]{:S(2)}, u32[]{:S(2)}) collective-permute-start(bf16[16,2,128,128]{3,2,1,0:T(8,128)(2,1)} %collective-permute-done.11.rest_7_), channel_id=1, source_target_pairs={{0,4},{4,0},{8,12},{12,8},{16,20},{20,16},{24,28},{28,24},{1,5},{5... | collective-permute-start | bytes 3145736 | tf_op jit(solution)/shard_map/ppermute | solution.py:1001
  95.7 23.6 %collective-permute-start.12 = (bf16[2048,256]{1,0:T(8,128)(2,1)}, bf16[2048,256]{1,0:T(8,128)(2,1)}, u32[]{:S(2)}, u32[]{:S(2)}) collective-permute-start(bf16[2048,256]{1,0:T(8,128)(2,1)} %get-tuple-element.155), channel_id=1, source_target_pairs={{0,8},{8,16},{16,24},{12,4},{20,12},{28,20},{1,9},{9,17},{17,25},{... | collective-permute-start | bytes 3145736 | tf_op jit(solution)/shard_map/ppermute | solution.py:901
  101.7 22.6 %collective-permute-start.20 = (bf16[2048,256]{1,0:T(8,128)(2,1)}, bf16[2048,256]{1,0:T(8,128)(2,1)S(1)}, u32[]{:S(2)}, u32[]{:S(2)}) collective-permute-start(bf16[2048,256]{1,0:T(8,128)(2,1)} %get-tuple-element.156), channel_id=1, source_target_pairs={{0,8},{8,16},{16,24},{12,4},{20,12},{28,20},{1,9},{9,17},{17,25},{... | collective-permute-start | bytes 3145736 | tf_op jit(solution)/shard_map/ppermute | solution.py:901
  105.2 1.0 copy-start.5
  120.0 18.2 %collective-permute-start.21 = (bf16[2048,256]{1,0:T(8,128)(2,1)}, bf16[2048,256]{1,0:T(8,128)(2,1)S(1)}, u32[]{:S(2)}, u32[]{:S(2)}) collective-permute-start(bf16[2048,256]{1,0:T(8,128)(2,1)} %take_states.12), channel_id=1, source_target_pairs={{0,8},{8,16},{16,24},{12,4},{20,12},{28,20},{1,9},{9,17},{17,25},{... | collective-permute-start | bytes 3145736 | tf_op jit(solution)/shard_map/ppermute | solution.py:901
  121.4 10.8 %copy-start.6 = (bf16[1024,128]{1,0:T(8,128)(2,1)S(1)}, bf16[1024,128]{1,0:T(8,128)(2,1)}, u32[]{:S(2)}) copy-start(bf16[1024,128]{1,0:T(8,128)(2,1)} %get-tuple-element.209.ks_ref) | copy-start | bytes 786436
  124.3 33.7 %copy-start.21 = (bf16[2048,256]{1,0:T(8,128)(2,1)}, bf16[2048,256]{1,0:T(8,128)(2,1)S(1)}, u32[]{:S(2)}) copy-start(bf16[2048,256]{1,0:T(8,128)(2,1)S(1)} %collective-permute-done.20.rest_5_.rest_7_) | copy-start | bytes 3145732
  124.9 21.8 %collective-permute-start.22 = (bf16[2048,256]{1,0:T(8,128)(2,1)}, bf16[2048,256]{1,0:T(8,128)(2,1)}, u32[]{:S(2)}, u32[]{:S(2)}) collective-permute-start(bf16[2048,256]{1,0:T(8,128)(2,1)} %take_states.13), channel_id=1, source_target_pairs={{0,8},{8,16},{16,24},{12,4},{20,12},{28,20},{1,9},{9,17},{17,25},{... | collective-permute-start | bytes 3145736 | tf_op jit(solution)/shard_map/ppermute | solution.py:901
  138.2 19.8 %copy-start.23 = (bf16[2048,256]{1,0:T(8,128)(2,1)}, bf16[2048,256]{1,0:T(8,128)(2,1)S(1)}, u32[]{:S(2)}) copy-start(bf16[2048,256]{1,0:T(8,128)(2,1)S(1)} %collective-permute-done.21.rest_6_.rest_8_) | copy-start | bytes 3145732
  138.8 19.2 %collective-permute-start.23 = (bf16[2048,256]{1,0:T(8,128)(2,1)}, bf16[2048,256]{1,0:T(8,128)(2,1)}, u32[]{:S(2)}, u32[]{:S(2)}) collective-permute-start(bf16[2048,256]{1,0:T(8,128)(2,1)} %take_states.14), channel_id=1, source_target_pairs={{0,8},{8,16},{16,24},{12,4},{20,12},{28,20},{1,9},{9,17},{17,25},{... | collective-permute-start | bytes 3145736 | tf_op jit(solution)/shard_map/ppermute | solution.py:901
  147.4 24.0 %collective-permute-start.24 = (bf16[2048,256]{1,0:T(8,128)(2,1)}, bf16[2048,256]{1,0:T(8,128)(2,1)}, u32[]{:S(2)}, u32[]{:S(2)}) collective-permute-start(bf16[2048,256]{1,0:T(8,128)(2,1)} %take_states.15), channel_id=1, source_target_pairs={{0,8},{8,16},{16,24},{12,4},{20,12},{28,20},{1,9},{9,17},{17,25},{... | collective-permute-start | bytes 3145736 | tf_op jit(solution)/shard_map/ppermute | solution.py:901
  158.7 21.8 %collective-permute-start.25 = (bf16[2048,256]{1,0:T(8,128)(2,1)}, bf16[2048,256]{1,0:T(8,128)(2,1)}, u32[]{:S(2)}, u32[]{:S(2)}) collective-permute-start(bf16[2048,256]{1,0:T(8,128)(2,1)} %take_states.16), channel_id=1, source_target_pairs={{0,8},{8,16},{16,24},{12,4},{20,12},{28,20},{1,9},{9,17},{17,25},{... | collective-permute-start | bytes 3145736 | tf_op jit(solution)/shard_map/ppermute | solution.py:901
  164.8 0.9 copy-start.7
  181.1 7.6 %copy-start.2 = (bf16[1024,2048]{1,0:T(8,128)(2,1)S(1)}, bf16[1024,2048]{1,0:T(8,128)(2,1)}, u32[]{:S(2)}) copy-start(bf16[1024,2048]{1,0:T(8,128)(2,1)} %get-tuple-element.168.rest_17_) | copy-start | bytes 12582916
  181.1 7.6 %copy-start.4 = (bf16[1024,256]{1,0:T(8,128)(2,1)S(1)}, bf16[1024,256]{1,0:T(8,128)(2,1)}, u32[]{:S(2)}) copy-start(bf16[1024,256]{1,0:T(8,128)(2,1)} %get-tuple-element.206.c_ref.rest_15_) | copy-start | bytes 1572868
  181.1 7.6 %copy-start.9 = (bf16[128,2048]{1,0:T(8,128)(2,1)S(1)}, bf16[128,2048]{1,0:T(8,128)(2,1)}, u32[]{:S(2)}) copy-start(bf16[128,2048]{1,0:T(8,128)(2,1)} %constant.87.clone.spread_ref.rest_19_) | copy-start | bytes 1572868
  181.1 7.5 %copy-start.11 = (bf16[1024,128]{1,0:T(8,128)(2,1)S(1)}, bf16[1024,128]{1,0:T(8,128)(2,1)}, u32[]{:S(2)}) copy-start(bf16[1024,128]{1,0:T(8,128)(2,1)} %copy-done.10) | copy-start | bytes 786436
  181.1 7.5 %copy-start.16 = (f32[16,128]{1,0:T(8,128)S(1)}, f32[16,128]{1,0:T(8,128)}, u32[]{:S(2)}) copy-start(f32[16,128]{1,0:T(8,128)} %copy-done.15) | copy-start | bytes 24580
  181.1 7.5 %copy-start.17 = (f32[2048]{0:T(1024)S(1)}, f32[2048]{0:T(1024)}, u32[]{:S(2)}) copy-start(f32[2048]{0:T(1024)} %param.29) | copy-start | bytes 24580
  181.9 13.7 %collective-permute-start.26 = (bf16[4,2048,256]{2,1,0:T(8,128)(2,1)}, bf16[4,2048,256]{2,1,0:T(8,128)(2,1)S(1)}, u32[]{:S(2)}, u32[]{:S(2)}) collective-permute-start(bf16[4,2048,256]{2,1,0:T(8,128)(2,1)} %pick_states.1), channel_id=1, source_target_pairs={{0,4},{4,0},{8,12},{12,8},{16,20},{20,16},{24,28},{28,24},{1,5},{5... | collective-permute-start | bytes 12582920 | tf_op jit(solution)/shard_map/ppermute | solution.py:1033
  188.7 7.0 %copy-start.20 = (bf16[4,2048,256]{2,1,0:T(8,128)(2,1)S(1)}, bf16[4,2048,256]{2,1,0:T(8,128)(2,1)}, u32[]{:S(2)}) copy-start(bf16[4,2048,256]{2,1,0:T(8,128)(2,1)} %get-tuple-element.387) | copy-start | bytes 12582916
  188.7 7.0 %copy-start.22 = (bf16[2048,256]{1,0:T(8,128)(2,1)S(1)}, bf16[2048,256]{1,0:T(8,128)(2,1)}, u32[]{:S(2)}) copy-start(bf16[2048,256]{1,0:T(8,128)(2,1)} %get-tuple-element.389) | copy-start | bytes 3145732
  195.6 11.4 %copy-start.1 = (bf16[1024,2,4,128]{3,2,1,0:T(4,128)(2,1)S(1)}, bf16[1024,2,4,128]{3,2,1,0:T(4,128)(2,1)}, u32[]{:S(2)}) copy-start(bf16[1024,2,4,128]{3,2,1,0:T(4,128)(2,1)} %param.26) | copy-start | bytes 6291460
where the time goes:
time: 207 us
  Pallas kernels  80.2 us (39%)
  starting transfers between devices  76.6 us (37%)
  waiting for transfers between devices  29.9 us (14%)
  local copies, waits for them, and re-layouts  17.6 us (9%)
    ppermute x11, starting transfers between devices, send(): return lax.ppermute(item, 'owner', up + down)  52.6 us
    pallas_call x4, Pallas kernels, attention(): pl.pallas_call(functools.partial(attend_kernel, qheads, (len(parts) + 2)...  29.3 us
    ppermute x11, waiting for transfers between devices, send(): return lax.ppermute(item, 'owner', up + down)  24.1 us
    pallas_call x2, Pallas kernels, mamba_pre(): pl.pallas_call(functools.partial(mamba_pre_kernel, heads), grid_spec=pltp...  20.5 us
    ppermute x6, starting transfers between devices, body(): got = [lax.ppermute(piece, 'owner', line(hop)) for piece in pieces]  14.1 us
    pallas_call x2, Pallas kernels, mamba_post(): pl.pallas_call(functools.partial(mamba_post_kernel, heads, whole_group, c...  13.9 us
    dynamic_slice x6, local copies, waits for them, and re-layouts, head_of(): return lax.dynamic_index_in_dim(array, index, axis, keepdims=False)  11.6 us
    pallas_call x8, Pallas kernels, take(): pl.pallas_call(functools.partial(take_kernel, states, steps, late is not...  11.5 us
  transfers between devices with their start and end apart: 26, of which 7 were waited for; matrix products, arithmetic and copies ran while one was open for 8% of the time, Pallas kernels for 33%

commit v1 on v0

--- a/solution.py
+++ b/solution.py
@@ -230,12 +230,18 @@
         pltpu.make_async_copy(piece_of(src, k), piece_of(dst, k), sems.at[k]).wait()
 
 
+def each_step(refs):
+    return [part for ref in refs for part in ([ref.at[k] for k in range(ref.shape[0])] if len(ref.shape) == 3 else [ref])]
+
+
 def take_kernel(states, steps, late, here_ref, table_ref, step_ref, pool_ref, near_ref, *rest):
-    sends, (item_ref, sem) = rest[-2 - steps : -2], rest[-2:]
-    came_refs = rest[: -2 - steps]
+    send_ref, item_ref, sem = rest[-3:]
+    sends = each_step([send_ref])
+    came_refs = rest[:-3]
     late_ref = None
     if late:
         came_refs, late_ref = came_refs[:-1], came_refs[-1]
+    came_refs = each_step(came_refs)
     codes = [table_ref[step_ref[0] + t] for t in range(steps)]
     for t in range(steps):
         start_from(
@@ -250,7 +256,7 @@
 
 
 def take(states, steps, here, table, step, pool, near, came, late=None):
-    item = jax.ShapeDtypeStruct(pool.shape[1:], pool.dtype)
+    shape = pool.shape[1:] if steps == 1 else (steps,) + pool.shape[1:]
     came = list(came) + ([] if late is None else [late])
     return pl.pallas_call(
         functools.partial(take_kernel, states, steps, late is not None),
@@ -258,13 +264,13 @@
             num_scalar_prefetch=3,
             grid=(1,),
             in_specs=[IN_HBM] * (2 + len(came)),
-            out_specs=[IN_HBM] * steps,
+            out_specs=IN_HBM,
             scratch_shapes=[
                 pltpu.VMEM((steps,) + pool.shape[1:], pool.dtype),
                 pltpu.SemaphoreType.DMA((steps, PIECES)),
             ],
         ),
-        out_shape=[item] * steps,
+        out_shape=jax.ShapeDtypeStruct(shape, pool.dtype),
         compiler_params=pltpu.CompilerParams(vmem_limit_bytes=SMALL_VMEM),
         name="take_states",
     )(here, table, step, pool, near, *came)
@@ -311,7 +317,7 @@
 
 
 def pick_kernel(states, cap, count, table_ref, *rest):
-    came_refs, late_ref = rest[:-4], rest[-4]
+    came_refs, late_ref = each_step(rest[:-4]), rest[-4]
     out_ref, item_ref, sem = rest[-3:]
     codes = [table_ref[2 * cap + 3 + 2 * count + r] for r in range(count)]
     for r in range(count):
@@ -519,6 +525,7 @@
 ):
     outs = 1 if whole_group else 2
     pool_ref, near_ref, *came_refs, late_ref, other_ref = rest[: fixed + 4]
+    came_refs = each_step(came_refs)
     c_ref, pre_ref, z_ref, e_ref, spread_ref, gain_ref, *rest = rest[fixed + 4 :]
     out_refs = rest[outs : 2 * outs]
     stage_refs = rest[2 * outs : 3 * outs]
@@ -989,10 +996,8 @@
             done = (table, near)
         else:
             step = HOP_STEPS * (hop - 2)
-            items = take(states, HOP_STEPS, here, table, step_at(step), pool, near, came)
-            items = [after(item, piece) for item, piece in zip(items, pieces)]
-            came += [send(item, step + k) for k, item in enumerate(items)]
-            tie = items[0]
+            tie = after(take(states, HOP_STEPS, here, table, step_at(step), pool, near, came), pieces[0])
+            came.append(send(tie, step))
             done = ()
         if beside:
             done += beside.pop(0)(tie)
@@ -1004,15 +1009,16 @@
     beside += [attention_part(r) for r in range(count)]
     started = HOP_STEPS * (chips - 2)
     fixed = started + FREE_STEPS
-    items = take(states, LAG, after(here, pieces[1]), table, step_at(started), pool, near, came)
-    flying = [send(item, started + k) for k, item in enumerate(items)]
-    tie = items[-1]
+    flying = []
+    for step in range(started, started + LAG):
+        tie = take(states, 1, after(here, pieces[1]), table, step_at(step), pool, near, came)
+        flying.append(send(tie, step))
     for step in range(started + LAG, fixed):
         done = ()
         if (step - started) % 2 == 0 and beside:
             done = beside.pop(0)(tie)
         came.append(after(flying.pop(0), *done))
-        (item,) = take(states, 1, here, table, step_at(step), pool, near, came)
+        item = take(states, 1, here, table, step_at(step), pool, near, came)
         flying.append(send(item, step))
         tie = item
     done = ()
@@ -1023,7 +1029,7 @@
     came.append(flying[1])
 
     def more(step, room):
-        (item,) = take(states, 1, here, table, step.reshape(1), pool, near, came, room)
+        item = take(states, 1, here, table, step.reshape(1), pool, near, came, room)
         return keep(fixed, step.reshape(1), send(item, fixed), room)
 
     room = blank(here, (cap - fixed,) + pool.shape[1:], pool.dtype)

time: 207 us -> 226 us (1.092)
  waiting for transfers between devices: 29.9 us -> 45.3 us
  starting transfers between devices: 76.6 us -> 61.8 us
  Pallas kernels: 80.2 us -> 92.9 us
  local copies, waits for them, and re-layouts: 17.6 us -> 23.7 us
    ppermute x6, waiting for transfers between devices: 1.38 us -> 30.2 us  [body(): got = [lax.ppermute(piece, 'owner', line(hop)) for piece in pieces]]
    ppermute x11 -> x9, waiting for transfers between devices: 24.1 us -> 10.7 us  [send(): return lax.ppermute(item, 'owner', up + down)]
    pallas_call x4, Pallas kernels: 29.3 us -> 41.3 us  [attention(): pl.pallas_call(functools.partial(attend_kernel, qheads, (len(parts) + 2)...]
    ppermute x11 -> x9, starting transfers between devices: 52.6 us -> 41.3 us  [send(): return lax.ppermute(item, 'owner', up + down)]
    unnamed x60 -> x66, local copies, waits for them, and re-layouts: 2.03 us -> 6.08 us
    pallas_call x8 -> x9, Pallas kernels: 11.5 us -> 12.1 us  [take(): pl.pallas_call(functools.partial(take_kernel, states, steps, late is not...]
  transfers between devices with their start and end apart: 26 -> 24, of which waited for: 7 -> 6; matrix products, arithmetic and copies ran while one was open for 8% -> 8% of each run, Pallas kernels for 33% -> 34%
where the time goes in v1:
time: 226 us; the launch traced here: 227 us
  Pallas kernels  92.9 us (41%)
  starting transfers between devices  61.8 us (27%)
  waiting for transfers between devices  45.3 us (20%)
  local copies, waits for them, and re-layouts  23.7 us (10%)
    pallas_call x4, Pallas kernels, attention(): pl.pallas_call(functools.partial(attend_kernel, qheads, (len(parts) + 2)...  41.3 us
    ppermute x9, starting transfers between devices, send(): return lax.ppermute(item, 'owner', up + down)  41.3 us
    ppermute x6, waiting for transfers between devices, body(): got = [lax.ppermute(piece, 'owner', line(hop)) for piece in pieces]  30.2 us
    pallas_call x2, Pallas kernels, mamba_pre(): pl.pallas_call(functools.partial(mamba_pre_kernel, heads), grid_spec=pltp...  20.5 us
    pallas_call x2, Pallas kernels, mamba_post(): pl.pallas_call(functools.partial(mamba_post_kernel, heads, whole_group, c...  13.9 us
    ppermute x6, starting transfers between devices, body(): got = [lax.ppermute(piece, 'owner', line(hop)) for piece in pieces]  12.8 us
    pallas_call x9, Pallas kernels, take(): pl.pallas_call(functools.partial(take_kernel, states, steps, late is not...  12.1 us
    dynamic_slice x6, local copies, waits for them, and re-layouts, head_of(): return lax.dynamic_index_in_dim(array, index, axis, keepdims=False)  11.6 us
  transfers between devices with their start and end apart: 24, of which 6 were waited for; matrix products, arithmetic and copies ran while one was open for 8% of the time, Pallas kernels for 34%

profile of v1, /device:TPU:0, one launch (start us, length us, event | category | flops | bytes accessed | tf_op | source)
XLA Modules:
  0.0 226.6 jit_solution(12764503095282459879)
XLA Ops:
  0.7 0.5 collective-permute-start.2
  1.2 4.7 %constant_dynamic-slice_fusion.2 = bf16[16,128,2,1,128]{4,3,2,1,0:T(2,128)(2,1)S(1)} fusion(bf16[16,128,2,4,128]{4,3,2,1,0:T(4,128)(2,1)} %param.28, s32[]{:T(128)S(6)} %select_n.19), kind=kLoop, calls=%fused_computation.10 | loop fusion | bytes 2097156 | tf_op jit(solution)/shard_map/jit(dynamic_index_in_dim)/dynamic_slice | solution.py:911
  5.9 0.3 copy.41
  6.2 0.2 collective-permute-start.1
  6.4 5.8 %collective-permute-start.3 = (bf16[16,2,128,128]{3,2,1,0:T(8,128)(2,1)S(1)}, bf16[16,2,128,128]{3,2,1,0:T(8,128)(2,1)}, u32[]{:S(2)}, u32[]{:S(2)}) collective-permute-start(bf16[16,2,128,128]{3,2,1,0:T(8,128)(2,1)S(1)} %bitcast.34), channel_id=1, source_target_pairs={{0,8},{8,16},{16,24},{12,4},{20,12},{28,20},{1,9},{9,17},{17,25},{... | collective-permute-start | bytes 3145736 | tf_op jit(solution)/shard_map/ppermute | solution.py:993
  12.2 0.5 bitcast_add_fusion.1.ids_ref
  12.7 4.3 %constant_dynamic-slice_fusion.1 = bf16[1024,2,1,256]{3,2,1,0:T(2,128)(2,1)S(1)} fusion(bf16[1024,2,4,256]{3,2,1,0:T(4,128)(2,1)} %param.24, s32[]{:T(128)S(6)} %select_n.21), kind=kLoop, calls=%fused_computation.9 | loop fusion | bytes 2097156 | tf_op jit(solution)/shard_map/jit(dynamic_index_in_dim)/dynamic_slice | solution.py:911
  17.0 1.1 copy.40
  18.2 1.1 constant_dynamic-slice_fusion
  19.4 4.3 %route_states.1.table_ref = s32[132]{0:T(256)S(1)} custom-call(s32[32]{0:T(128)} %bitcast_add_fusion.1.ids_ref, s32[1]{0:T(128)} %bitcast.1.here_ref), custom_call_target="tpu_custom_call" | custom-call | tf_op jit(solution)/shard_map/route_states/pallas_call | solution.py:165
  23.7 0.7 slice_bitcast_fusion.2
  24.5 2.2 slice_bitcast_fusion
  26.7 2.9 %take_states.10 = bf16[2,2048,256]{2,1,0:T(8,128)(2,1)} custom-call(s32[1]{0:T(128)} %bitcast.1.here_ref, s32[132]{0:T(256)S(1)} %route_states.1.table_ref, s32[1]{0:T(128)} %constant.71.clone.1.step_ref, bf16[4,2048,256]{2,1,0:T(8,128)(2,1)} %bitcast.44, bf16[4,2048,256]{2,1,0:T(8,128)(2,1)} %collective-permute-done.2.near_ref.rest_1_), custom_call_target="tpu_custom_call" | custom-call | tf_op jit(solution)/shard_map/take_states/pallas_call | solution.py:261
  29.6 2.6 %collective-permute-start.4 = (bf16[2,2048,256]{2,1,0:T(8,128)(2,1)}, bf16[2,2048,256]{2,1,0:T(8,128)(2,1)}, u32[]{:S(2)}, u32[]{:S(2)}) collective-permute-start(bf16[2,2048,256]{2,1,0:T(8,128)(2,1)} %take_states.10), channel_id=1, source_target_pairs={{0,8},{28,20},{1,9},{29,21},{2,10},{30,22},{3,11},{31,23}} | collective-permute-start | bytes 6291464 | tf_op jit(solution)/shard_map/ppermute | solution.py:908
  32.3 1.3 collective-permute-start.7
  33.6 0.7 collective-permute-start.5
  34.4 0.7 broadcast_in_dim.17
  35.0 0.8 broadcast_in_dim_reshape.3.skip_ref
  35.8 30.2 %collective-permute-done.7.rest_3_ = bf16[16,2,128,128]{3,2,1,0:T(8,128)(2,1)S(1)} collective-permute-done((bf16[16,2,128,128]{3,2,1,0:T(8,128)(2,1)}, bf16[16,2,128,128]{3,2,1,0:T(8,128)(2,1)S(1)}, u32[]{:S(2)}, u32[]{:S(2)}) %collective-permute-start.7) | collective-permute-done | bytes 1048608 | tf_op jit(solution)/shard_map/ppermute | solution.py:993
  66.0 1.6 collective-permute-start.8
  67.6 0.7 broadcast_in_dim.16.decay_ref
  68.4 1.0 copy-done.3
  69.4 1.0 copy-done.8
  70.5 1.0 copy-done.13
  71.5 0.9 copy-done.16
  72.4 9.5 %mamba_pre.2 = (f32[1024,2048]{1,0:T(8,128)}, bf16[1024,2048]{1,0:T(8,128)(2,1)}, bf16[1024,128]{1,0:T(8,128)(2,1)S(1)}) custom-call(s32[32]{0:T(128)S(1)} %copy-done.21, s32[1]{0:T(128)} %bitcast.11.first_ref, bf16[1024,2,2048]{2,1,0:T(2,128)(2,1)} %mix_ref.3, bf16[1024,256]{1,0:T(8,128)(2,1)S(1)} %copy-done.13, bf16[1024,256]{1,0:T(8,128)(2,1)S(1)} %copy-done.3, ...), custom_call_target="tpu_custom_call" | custom-call | flops 5368709120 | bytes 10485760 | tf_op jit(solution)/shard_map/mamba_pre/pallas_call | solution.py:473
  82.0 2.9 %take_states.11 = bf16[2,2048,256]{2,1,0:T(8,128)(2,1)} custom-call(s32[1]{0:T(128)} %bitcast.1.here_ref, s32[132]{0:T(256)S(1)} %route_states.1.table_ref, s32[1]{0:T(128)} %constant.75.clone.1.step_ref, bf16[4,2048,256]{2,1,0:T(8,128)(2,1)} %bitcast.45, bf16[4,2048,256]{2,1,0:T(8,128)(2,1)} %collective-permute-done.2.near_ref.rest_1_, ...), custom_call_target="tpu_custom_call" | custom-call | tf_op jit(solution)/shard_map/take_states/pallas_call | solution.py:261
  84.9 6.3 %collective-permute-start.6 = (bf16[2,2048,256]{2,1,0:T(8,128)(2,1)}, bf16[2,2048,256]{2,1,0:T(8,128)(2,1)}, u32[]{:S(2)}, u32[]{:S(2)}) collective-permute-start(bf16[2,2048,256]{2,1,0:T(8,128)(2,1)} %take_states.11), channel_id=1, source_target_pairs={{0,8},{8,16},{20,12},{28,20},{1,9},{9,17},{21,13},{29,21},{2,10},{... | collective-permute-start | bytes 6291464 | tf_op jit(solution)/shard_map/ppermute | solution.py:908
  91.2 1.7 collective-permute-start.11
  92.9 1.6 collective-permute-start.9
  94.5 0.5 collective-permute-start.12
  95.0 11.0 %mamba_pre.3 = (f32[1024,2048]{1,0:T(8,128)}, bf16[1024,2048]{1,0:T(8,128)(2,1)}, bf16[1024,128]{1,0:T(8,128)(2,1)S(1)}) custom-call(s32[32]{0:T(128)S(1)} %copy-done.21, s32[1]{0:T(128)S(6)} %add.36.first_ref, bf16[1024,2,2048]{2,1,0:T(2,128)(2,1)} %mix_ref.3, ...), custom_call_target="tpu_custom_call", output_to_operand_aliasing={{0}: (10, {}), {1}: (11, {}), {2}: (12, {})} | custom-call | flops 5368709120 | bytes 10485760 | tf_op jit(solution)/shard_map/mamba_pre/pallas_call | solution.py:473
  106.1 0.5 collective-permute-start.14
  106.6 1.0 copy-done.28
  107.7 6.0 %collective-permute-done.6.rest_1_.rest_3_ = bf16[2,2048,256]{2,1,0:T(8,128)(2,1)} collective-permute-done((bf16[2,2048,256]{2,1,0:T(8,128)(2,1)}, bf16[2,2048,256]{2,1,0:T(8,128)(2,1)}, u32[]{:S(2)}, u32[]{:S(2)}) %collective-permute-start.6) | collective-permute-done | bytes 2097184 | tf_op jit(solution)/shard_map/ppermute | solution.py:908
  113.7 2.5 %take_states.12 = bf16[2048,256]{1,0:T(8,128)(2,1)} custom-call(s32[1]{0:T(128)} %bitcast.1.here_ref, s32[132]{0:T(256)S(1)} %route_states.1.table_ref, s32[1]{0:T(128)} %constant.77.clone.1.step_ref, bf16[4,2048,256]{2,1,0:T(8,128)(2,1)} %bitcast.46, bf16[4,2048,256]{2,1,0:T(8,128)(2,1)} %collective-permute-done.2.near_ref.rest_1_, ...), custom_call_target="tpu_custom_call" | custom-call | tf_op jit(solution)/shard_map/take_states/pallas_call | solution.py:261
  116.2 5.4 %collective-permute-start.10 = (bf16[2048,256]{1,0:T(8,128)(2,1)}, bf16[2048,256]{1,0:T(8,128)(2,1)}, u32[]{:S(2)}, u32[]{:S(2)}) collective-permute-start(bf16[2048,256]{1,0:T(8,128)(2,1)} %take_states.12), channel_id=1, source_target_pairs={{0,8},{8,16},{16,24},{12,4},{20,12},{28,20},{1,9},{9,17},{17,25},{... | collective-permute-start | bytes 3145736 | tf_op jit(solution)/shard_map/ppermute | solution.py:908
  121.9 0.6 take_states.13
  122.5 3.8 %collective-permute-start.18 = (bf16[2048,256]{1,0:T(8,128)(2,1)}, bf16[2048,256]{1,0:T(8,128)(2,1)S(1)}, u32[]{:S(2)}, u32[]{:S(2)}) collective-permute-start(bf16[2048,256]{1,0:T(8,128)(2,1)} %take_states.13), channel_id=1, source_target_pairs={{0,8},{8,16},{16,24},{12,4},{20,12},{28,20},{1,9},{9,17},{17,25},{... | collective-permute-start | bytes 3145736 | tf_op jit(solution)/shard_map/ppermute | solution.py:908
  126.4 13.2 %attention.4.rest_14_ = bf16[1024,1024]{1,0:T(8,128)(2,1)} custom-call(s32[2]{0:T(128)S(1)} %pad_add_fusion.first_ref, s32[512]{0:T(512)S(1)} %reshape.29.pages_ref, s32[32]{0:T(128)S(1)} %copy-done.22, s32[32]{0:T(128)S(1)} %copy-done.21, bf16[1024,1024]{1,0:T(8,128)(2,1)} %q_ref.7, bf16[1024,128]{1,0:T(8,128)(2,1)S(1)} %copy-done.6, ...), custom_call_target="tpu_custom_call" | custom-call | flops 2415919104 | bytes 2097152 | tf_op jit(solution)/shard_map/attention/pallas_call | solution.py:826
  139.6 0.6 take_states.14
  140.2 1.4 collective-permute-start.19
  141.7 2.8 %collective-permute-done.18.rest_3_.rest_5_ = bf16[2048,256]{1,0:T(8,128)(2,1)S(1)} collective-permute-done((bf16[2048,256]{1,0:T(8,128)(2,1)}, bf16[2048,256]{1,0:T(8,128)(2,1)S(1)}, u32[]{:S(2)}, u32[]{:S(2)}) %collective-permute-start.18) | collective-permute-done | bytes 1048608 | tf_op jit(solution)/shard_map/ppermute | solution.py:908
  144.5 0.6 take_states.15
  145.1 7.2 %collective-permute-start.20 = (bf16[2048,256]{1,0:T(8,128)(2,1)}, bf16[2048,256]{1,0:T(8,128)(2,1)}, u32[]{:S(2)}, u32[]{:S(2)}) collective-permute-start(bf16[2048,256]{1,0:T(8,128)(2,1)} %take_states.15), channel_id=1, source_target_pairs={{0,8},{8,16},{16,24},{12,4},{20,12},{28,20},{1,9},{9,17},{17,25},{... | collective-permute-start | bytes 3145736 | tf_op jit(solution)/shard_map/ppermute | solution.py:908
  152.3 6.7 %attention.5.rest_14_ = bf16[1024,1024]{1,0:T(8,128)(2,1)} custom-call(s32[2]{0:T(128)S(1)} %pad_add_fusion.1.first_ref, s32[512]{0:T(512)S(1)} %reshape.29.pages_ref, s32[32]{0:T(128)S(1)} %copy-done.22, s32[32]{0:T(128)S(1)} %copy-done.21, bf16[1024,1024]{1,0:T(8,128)(2,1)} %q_ref.7, ...), custom_call_target="tpu_custom_call", output_to_operand_aliasing={{}: (21, {})} | custom-call | flops 2415919104 | bytes 2097152 | tf_op jit(solution)/shard_map/attention/pallas_call | solution.py:826
  159.0 0.6 take_states.16
  159.7 6.8 %collective-permute-start.21 = (bf16[2048,256]{1,0:T(8,128)(2,1)}, bf16[2048,256]{1,0:T(8,128)(2,1)}, u32[]{:S(2)}, u32[]{:S(2)}) collective-permute-start(bf16[2048,256]{1,0:T(8,128)(2,1)} %take_states.16), channel_id=1, source_target_pairs={{0,8},{8,16},{16,24},{12,4},{20,12},{28,20},{1,9},{9,17},{17,25},{... | collective-permute-start | bytes 3145736 | tf_op jit(solution)/shard_map/ppermute | solution.py:908
  166.6 0.3 collective-permute-done.20.rest_5_.rest_7_
  166.9 0.6 take_states.17
  167.6 5.4 %collective-permute-start.22 = (bf16[2048,256]{1,0:T(8,128)(2,1)}, bf16[2048,256]{1,0:T(8,128)(2,1)}, u32[]{:S(2)}, u32[]{:S(2)}) collective-permute-start(bf16[2048,256]{1,0:T(8,128)(2,1)} %take_states.17), channel_id=1, source_target_pairs={{0,8},{8,16},{16,24},{12,4},{20,12},{28,20},{1,9},{9,17},{17,25},{... | collective-permute-start | bytes 3145736 | tf_op jit(solution)/shard_map/ppermute | solution.py:908
  173.0 11.5 %attention.6.rest_14_ = bf16[1024,1024]{1,0:T(8,128)(2,1)} custom-call(s32[2]{0:T(128)S(1)} %pad_add_fusion.2.first_ref, s32[512]{0:T(512)S(1)} %reshape.29.pages_ref, s32[32]{0:T(128)S(1)} %copy-done.22, s32[32]{0:T(128)S(1)} %copy-done.21, bf16[1024,1024]{1,0:T(8,128)(2,1)} %q_ref.7, ...), custom_call_target="tpu_custom_call", output_to_operand_aliasing={{}: (21, {})} | custom-call | flops 2415919104 | bytes 2097152 | tf_op jit(solution)/shard_map/attention/pallas_call | solution.py:826
  184.5 0.6 take_states.18
  185.2 2.3 %collective-permute-start.23 = (bf16[2048,256]{1,0:T(8,128)(2,1)}, bf16[2048,256]{1,0:T(8,128)(2,1)}, u32[]{:S(2)}, u32[]{:S(2)}) collective-permute-start(bf16[2048,256]{1,0:T(8,128)(2,1)} %take_states.18), channel_id=1, source_target_pairs={{0,8},{8,16},{16,24},{12,4},{20,12},{28,20},{1,9},{9,17},{17,25},{... | collective-permute-start | bytes 3145736 | tf_op jit(solution)/shard_map/ppermute | solution.py:908
  187.6 0.6 slice.19
  188.2 0.9 copy-done.7
  189.2 9.9 %attention.7 = bf16[1024,1024]{1,0:T(8,128)(2,1)} custom-call(s32[2]{0:T(128)S(1)} %pad_add_fusion.3.first_ref, s32[512]{0:T(512)S(1)} %reshape.29.pages_ref, s32[32]{0:T(128)S(1)} %copy-done.22, s32[32]{0:T(128)S(1)} %copy-done.21, bf16[1024,1024]{1,0:T(8,128)(2,1)} %q_ref.7, bf16[1024,128]{1,0:T(8,128)(2,1)S(1)} %copy-done.7, ...), custom_call_target="tpu_custom_call", output_to_operand_aliasing={{}: (21, {})} | custom-call | flops 2415919104 | bytes 2097152 | tf_op jit(solution)/shard_map/attention/pallas_call | solution.py:826
  199.1 1.6 collective-permute-done.23.rest_8_.rest_10_
  200.7 0.6 while.10
  201.4 0.8 pick_states.1
  202.1 5.9 %collective-permute-start.24 = (bf16[4,2048,256]{2,1,0:T(8,128)(2,1)}, bf16[4,2048,256]{2,1,0:T(8,128)(2,1)S(1)}, u32[]{:S(2)}, u32[]{:S(2)}) collective-permute-start(bf16[4,2048,256]{2,1,0:T(8,128)(2,1)} %pick_states.1), channel_id=1, source_target_pairs={{0,4},{4,0},{8,12},{12,8},{16,20},{20,16},{24,28},{28,24},{1,5},{5... | collective-permute-start | bytes 12582920 | tf_op jit(solution)/shard_map/ppermute | solution.py:1039
  208.1 2.6 %mamba_post.2.rest_19_ = bf16[1024,2048]{1,0:T(8,128)(2,1)} custom-call(s32[1]{0:T(128)} %bitcast.1.here_ref, s32[132]{0:T(256)S(1)} %get-tuple-element.357, s32[32]{0:T(128)S(1)} %copy-done.21, bf16[4,2048,256]{2,1,0:T(8,128)(2,1)} %get-tuple-element.339, bf16[4,2048,256]{2,1,0:T(8,128)(2,1)} %collective-permute-done.2.near_ref.rest_1_, ...), custom_call_target="tpu_custom_call" | custom-call | flops 1073741824 | bytes 12582912 | tf_op jit(solution)/shard_map/mamba_post/pallas_call | solution.py:639
  210.7 4.4 %collective-permute-done.24.rest_12_ = bf16[4,2048,256]{2,1,0:T(8,128)(2,1)S(1)} collective-permute-done((bf16[4,2048,256]{2,1,0:T(8,128)(2,1)}, bf16[4,2048,256]{2,1,0:T(8,128)(2,1)S(1)}, u32[]{:S(2)}, u32[]{:S(2)}) %collective-permute-start.24) | collective-permute-done | bytes 4194336 | tf_op jit(solution)/shard_map/ppermute | solution.py:1039
  215.1 11.4 %mamba_post.3 = bf16[1024,2048]{1,0:T(8,128)(2,1)} custom-call(s32[1]{0:T(128)} %bitcast.1.here_ref, s32[132]{0:T(256)S(1)} %get-tuple-element.357, s32[32]{0:T(128)S(1)} %copy-done.21, bf16[4,2048,256]{2,1,0:T(8,128)(2,1)S(1)} %copy-done.23, bf16[4,2048,256]{2,1,0:T(8,128)(2,1)} %collective-permute-done.2.near_ref.rest_1_, ...), custom_call_target="tpu_custom_call", output_to_operand_aliasing={{}: (22, {})} | custom-call | flops 1073741824 | bytes 12582912 | tf_op jit(solution)/shard_map/mamba_post/pallas_call | solution.py:639
  (93 shorter events, 0.9 us)
Async XLA Ops:
  0.6 17.5 %copy-start = (bf16[1024,2,4,128]{3,2,1,0:T(4,128)(2,1)S(1)}, bf16[1024,2,4,128]{3,2,1,0:T(4,128)(2,1)}, u32[]{:S(2)}) copy-start(bf16[1024,2,4,128]{3,2,1,0:T(4,128)(2,1)} %param.26) | copy-start | bytes 6291460
  0.6 11.5 %copy-start.33 = (s32[32,1]{0,1:T(1,128)S(1)}, s32[32,1]{0,1:T(1,128)}, u32[]{:S(2)}) copy-start(s32[32,1]{0,1:T(1,128)} %param.30) | copy-start | bytes 388
  0.7 11.5 %copy-start.32 = (s32[32]{0:T(128)S(1)}, s32[32]{0:T(128)}, u32[]{:S(2)}) copy-start(s32[32]{0:T(128)} %param.31) | copy-start | bytes 388
  0.7 26.0 %collective-permute-start.2 = (bf16[4,2048,256]{2,1,0:T(8,128)(2,1)}, bf16[4,2048,256]{2,1,0:T(8,128)(2,1)}, u32[]{:S(2)}, u32[]{:S(2)}) collective-permute-start(bf16[4,2048,256]{2,1,0:T(8,128)(2,1)} %bitcast.43), channel_id=1, source_target_pairs={{0,4},{4,0},{8,12},{12,8},{16,20},{20,16},{24,28},{28,24},{1,5},{5... | collective-permute-start | bytes 12582920 | tf_op jit(solution)/shard_map/ppermute | solution.py:914
  6.2 6.5 %collective-permute-start.1 = (bf16[16,2,128,128]{3,2,1,0:T(8,128)(2,1)S(1)}, bf16[16,2,128,128]{3,2,1,0:T(8,128)(2,1)}, u32[]{:S(2)}, u32[]{:S(2)}) collective-permute-start(bf16[16,2,128,128]{3,2,1,0:T(8,128)(2,1)S(1)} %bitcast.33), channel_id=1, source_target_pairs={{0,4},{4,0},{8,12},{12,8},{16,20},{20,16},{24,28},{28,24},{1,5},{5... | collective-permute-start | bytes 3145736 | tf_op jit(solution)/shard_map/ppermute | solution.py:916
  6.4 20.3 %collective-permute-start.3 = (bf16[16,2,128,128]{3,2,1,0:T(8,128)(2,1)S(1)}, bf16[16,2,128,128]{3,2,1,0:T(8,128)(2,1)}, u32[]{:S(2)}, u32[]{:S(2)}) collective-permute-start(bf16[16,2,128,128]{3,2,1,0:T(8,128)(2,1)S(1)} %bitcast.34), channel_id=1, source_target_pairs={{0,8},{8,16},{16,24},{12,4},{20,12},{28,20},{1,9},{9,17},{17,25},{... | collective-permute-start | bytes 3145736 | tf_op jit(solution)/shard_map/ppermute | solution.py:993
  26.7 7.7 %copy-start.31 = (f32[32]{0:T(128)S(1)}, f32[32]{0:T(128)}, u32[]{:S(2)}) copy-start(f32[32]{0:T(128)} %param.23) | copy-start | bytes 388
  26.7 41.7 %copy-start.15 = (f32[1024,32]{0,1:T(8,128)S(1)}, f32[1024,32]{0,1:T(8,128)}, u32[]{:S(2)}) copy-start(f32[1024,32]{0,1:T(8,128)} %param.21) | copy-start | bytes 393220
  26.7 41.7 %copy-start.21 = (s32[32]{0:T(128)S(1)}, s32[32]{0:T(128)}, u32[]{:S(2)}) copy-start(s32[32]{0:T(128)} %live_ref.15) | copy-start | bytes 388
  29.6 52.4 %collective-permute-start.4 = (bf16[2,2048,256]{2,1,0:T(8,128)(2,1)}, bf16[2,2048,256]{2,1,0:T(8,128)(2,1)}, u32[]{:S(2)}, u32[]{:S(2)}) collective-permute-start(bf16[2,2048,256]{2,1,0:T(8,128)(2,1)} %take_states.10), channel_id=1, source_target_pairs={{0,8},{28,20},{1,9},{29,21},{2,10},{30,22},{3,11},{31,23}} | collective-permute-start | bytes 6291464 | tf_op jit(solution)/shard_map/ppermute | solution.py:908
  32.3 33.7 %collective-permute-start.7 = (bf16[16,2,128,128]{3,2,1,0:T(8,128)(2,1)}, bf16[16,2,128,128]{3,2,1,0:T(8,128)(2,1)S(1)}, u32[]{:S(2)}, u32[]{:S(2)}) collective-permute-start(bf16[16,2,128,128]{3,2,1,0:T(8,128)(2,1)} %collective-permute-done.1.rest_1_), channel_id=1, source_target_pairs={{0,8},{8,16},{16,24},{12,4},{20,12},{28,20},{1,9},{9,17},{17,25},{... | collective-permute-start | bytes 3145736 | tf_op jit(solution)/shard_map/ppermute | solution.py:993
  33.6 48.3 %collective-permute-start.5 = (bf16[16,2,128,128]{3,2,1,0:T(8,128)(2,1)}, bf16[16,2,128,128]{3,2,1,0:T(8,128)(2,1)S(1)}, u32[]{:S(2)}, u32[]{:S(2)}) collective-permute-start(bf16[16,2,128,128]{3,2,1,0:T(8,128)(2,1)} %collective-permute-done.3.rest_2_), channel_id=1, source_target_pairs={{8,16},{16,24},{12,4},{20,12},{9,17},{17,25},{13,5},{21,13},{10,18... | collective-permute-start | bytes 3145736 | tf_op jit(solution)/shard_map/ppermute | solution.py:993
  66.0 26.8 %collective-permute-start.8 = (bf16[16,2,128,128]{3,2,1,0:T(8,128)(2,1)S(1)}, bf16[16,2,128,128]{3,2,1,0:T(8,128)(2,1)}, u32[]{:S(2)}, u32[]{:S(2)}) collective-permute-start(bf16[16,2,128,128]{3,2,1,0:T(8,128)(2,1)S(1)} %collective-permute-done.7.rest_3_), channel_id=1, source_target_pairs={{8,16},{16,24},{12,4},{20,12},{9,17},{17,25},{13,5},{21,13},{10,18... | collective-permute-start | bytes 3145736 | tf_op jit(solution)/shard_map/ppermute | solution.py:993
  68.4 1.0 copy-start.3
  69.4 1.0 copy-start.8
  70.5 1.0 copy-start.13
  71.5 0.9 copy-start.16
  72.4 9.5 %copy-start.18 = (f32[16,128]{1,0:T(8,128)}, f32[16,128]{1,0:T(8,128)S(1)}, u32[]{:S(2)}) copy-start(f32[16,128]{1,0:T(8,128)S(1)} %broadcast_1__pre_in__z_in__e_in_rest_19_.2._pre_in._z_in._e_in.rest_19_) | copy-start | bytes 24580
  81.9 13.1 %copy-start.4 = (bf16[1024,256]{1,0:T(8,128)(2,1)S(1)}, bf16[1024,256]{1,0:T(8,128)(2,1)}, u32[]{:S(2)}) copy-start(bf16[1024,256]{1,0:T(8,128)(2,1)} %get-tuple-element.176.c_ref.rest_13_) | copy-start | bytes 1572868
  82.0 13.1 %copy-start.9 = (bf16[128,2048]{1,0:T(8,128)(2,1)S(1)}, bf16[128,2048]{1,0:T(8,128)(2,1)}, u32[]{:S(2)}) copy-start(bf16[128,2048]{1,0:T(8,128)(2,1)} %constant.89.clone.spread_ref.rest_17_) | copy-start | bytes 1572868
  82.0 13.0 %copy-start.14 = (bf16[1024,256]{1,0:T(8,128)(2,1)S(1)}, bf16[1024,256]{1,0:T(8,128)(2,1)}, u32[]{:S(2)}) copy-start(bf16[1024,256]{1,0:T(8,128)(2,1)} %get-tuple-element.177.b_ref) | copy-start | bytes 1572868
  82.0 13.0 %copy-start.17 = (bf16[256,256]{1,0:T(8,128)(2,1)S(1)}, bf16[256,256]{1,0:T(8,128)(2,1)}, u32[]{:S(2)}) copy-start(bf16[256,256]{1,0:T(8,128)(2,1)} %constant.90.clone.split_ref) | copy-start | bytes 393220
  84.9 28.8 %collective-permute-start.6 = (bf16[2,2048,256]{2,1,0:T(8,128)(2,1)}, bf16[2,2048,256]{2,1,0:T(8,128)(2,1)}, u32[]{:S(2)}, u32[]{:S(2)}) collective-permute-start(bf16[2,2048,256]{2,1,0:T(8,128)(2,1)} %take_states.11), channel_id=1, source_target_pairs={{0,8},{8,16},{20,12},{28,20},{1,9},{9,17},{21,13},{29,21},{2,10},{... | collective-permute-start | bytes 6291464 | tf_op jit(solution)/shard_map/ppermute | solution.py:908
  91.2 14.8 %collective-permute-start.11 = (bf16[16,2,128,128]{3,2,1,0:T(8,128)(2,1)S(1)}, bf16[16,2,128,128]{3,2,1,0:T(8,128)(2,1)}, u32[]{:S(2)}, u32[]{:S(2)}) collective-permute-start(bf16[16,2,128,128]{3,2,1,0:T(8,128)(2,1)S(1)} %collective-permute-done.5.rest_4_), channel_id=1, source_target_pairs={{16,24},{12,4},{17,25},{13,5},{18,26},{14,6},{19,27},{15,7}} | collective-permute-start | bytes 3145736 | tf_op jit(solution)/shard_map/ppermute | solution.py:993
  92.9 13.3 %collective-permute-start.9 = (bf16[16,2,128,128]{3,2,1,0:T(8,128)(2,1)}, bf16[16,2,128,128]{3,2,1,0:T(8,128)(2,1)}, u32[]{:S(2)}, u32[]{:S(2)}) collective-permute-start(bf16[16,2,128,128]{3,2,1,0:T(8,128)(2,1)} %collective-permute-done.8.rest_5_), channel_id=1, source_target_pairs={{16,24},{12,4},{17,25},{13,5},{18,26},{14,6},{19,27},{15,7}} | collective-permute-start | bytes 3145736 | tf_op jit(solution)/shard_map/ppermute | solution.py:993
  94.5 12.1 %collective-permute-start.13 = (bf16[16,2,128,128]{3,2,1,0:T(8,128)(2,1)S(1)}, bf16[16,2,128,128]{3,2,1,0:T(8,128)(2,1)S(1)}, u32[]{:S(2)}, u32[]{:S(2)}) collective-permute-start(bf16[16,2,128,128]{3,2,1,0:T(8,128)(2,1)S(1)} %collective-permute-done.7.rest_3_), channel_id=1, source_target_pairs={{0,4},{4,0},{8,12},{12,8},{16,20},{20,16},{24,28},{28,24},{1,5},{5... | collective-permute-start | bytes 3145736 | tf_op jit(solution)/shard_map/ppermute | solution.py:1006
  94.5 21.7 %collective-permute-start.12 = (bf16[16,2,128,128]{3,2,1,0:T(8,128)(2,1)}, bf16[16,2,128,128]{3,2,1,0:T(8,128)(2,1)}, u32[]{:S(2)}, u32[]{:S(2)}) collective-permute-start(bf16[16,2,128,128]{3,2,1,0:T(8,128)(2,1)} %collective-permute-done.3.rest_2_), channel_id=1, source_target_pairs={{0,4},{4,0},{8,12},{12,8},{16,20},{20,16},{24,28},{28,24},{1,5},{5... | collective-permute-start | bytes 3145736 | tf_op jit(solution)/shard_map/ppermute | solution.py:1006
  106.0 10.2 %copy-start.11 = (bf16[1024,128]{1,0:T(8,128)(2,1)}, bf16[1024,128]{1,0:T(8,128)(2,1)S(1)}, u32[]{:S(2)}) copy-start(bf16[1024,128]{1,0:T(8,128)(2,1)S(1)} %get-tuple-element.128.rest_16_) | copy-start | bytes 786436
  106.0 15.6 %copy-start.29 = (s32[32,16]{0,1:T(8,128)S(1)}, s32[32,16]{0,1:T(8,128)}, u32[]{:S(2)}) copy-start(s32[32,16]{0,1:T(8,128)} %param.33) | copy-start | bytes 6148
  106.0 15.6 %copy-start.30 = (s32[32,16,1]{0,2,1:T(1,128)S(1)}, s32[32,16,1]{0,2,1:T(1,128)}, u32[]{:S(2)}) copy-start(s32[32,16,1]{0,2,1:T(1,128)} %param.32) | copy-start | bytes 6148
  106.0 16.5 %collective-permute-start.15 = (bf16[16,2,128,128]{3,2,1,0:T(8,128)(2,1)}, bf16[16,2,128,128]{3,2,1,0:T(8,128)(2,1)}, u32[]{:S(2)}, u32[]{:S(2)}) collective-permute-start(bf16[16,2,128,128]{3,2,1,0:T(8,128)(2,1)} %collective-permute-done.8.rest_5_), channel_id=1, source_target_pairs={{0,4},{4,0},{8,12},{12,8},{16,20},{20,16},{24,28},{28,24},{1,5},{5... | collective-permute-start | bytes 3145736 | tf_op jit(solution)/shard_map/ppermute | solution.py:1006
  106.1 20.2 %collective-permute-start.14 = (bf16[16,2,128,128]{3,2,1,0:T(8,128)(2,1)S(1)}, bf16[16,2,128,128]{3,2,1,0:T(8,128)(2,1)}, u32[]{:S(2)}, u32[]{:S(2)}) collective-permute-start(bf16[16,2,128,128]{3,2,1,0:T(8,128)(2,1)S(1)} %collective-permute-done.5.rest_4_), channel_id=1, source_target_pairs={{0,4},{4,0},{8,12},{12,8},{16,20},{20,16},{24,28},{28,24},{1,5},{5... | collective-permute-start | bytes 3145736 | tf_op jit(solution)/shard_map/ppermute | solution.py:1006
  106.6 1.0 copy-start.28
  107.6 18.8 %collective-permute-start.16 = (bf16[16,2,128,128]{3,2,1,0:T(8,128)(2,1)}, bf16[16,2,128,128]{3,2,1,0:T(8,128)(2,1)}, u32[]{:S(2)}, u32[]{:S(2)}) collective-permute-start(bf16[16,2,128,128]{3,2,1,0:T(8,128)(2,1)} %collective-permute-done.11.rest_6_), channel_id=1, source_target_pairs={{0,4},{4,0},{8,12},{12,8},{16,20},{20,16},{24,28},{28,24},{1,5},{5... | collective-permute-start | bytes 3145736 | tf_op jit(solution)/shard_map/ppermute | solution.py:1006
  113.7 12.7 %collective-permute-start.17 = (bf16[16,2,128,128]{3,2,1,0:T(8,128)(2,1)}, bf16[16,2,128,128]{3,2,1,0:T(8,128)(2,1)}, u32[]{:S(2)}, u32[]{:S(2)}) collective-permute-start(bf16[16,2,128,128]{3,2,1,0:T(8,128)(2,1)} %collective-permute-done.9.rest_7_), channel_id=1, source_target_pairs={{0,4},{4,0},{8,12},{12,8},{16,20},{20,16},{24,28},{28,24},{1,5},{5... | collective-permute-start | bytes 3145736 | tf_op jit(solution)/shard_map/ppermute | solution.py:1006
  116.2 23.4 %collective-permute-start.10 = (bf16[2048,256]{1,0:T(8,128)(2,1)}, bf16[2048,256]{1,0:T(8,128)(2,1)}, u32[]{:S(2)}, u32[]{:S(2)}) collective-permute-start(bf16[2048,256]{1,0:T(8,128)(2,1)} %take_states.12), channel_id=1, source_target_pairs={{0,8},{8,16},{16,24},{12,4},{20,12},{28,20},{1,9},{9,17},{17,25},{... | collective-permute-start | bytes 3145736 | tf_op jit(solution)/shard_map/ppermute | solution.py:908
  121.8 4.6 %copy-start.6 = (bf16[1024,128]{1,0:T(8,128)(2,1)S(1)}, bf16[1024,128]{1,0:T(8,128)(2,1)}, u32[]{:S(2)}) copy-start(bf16[1024,128]{1,0:T(8,128)(2,1)} %get-tuple-element.179.ks_ref) | copy-start | bytes 786436
  121.8 4.6 %copy-start.22 = (s32[32]{0:T(128)S(1)}, s32[32]{0:T(128)}, u32[]{:S(2)}) copy-start(s32[32]{0:T(128)} %prefix_ref.7) | copy-start | bytes 388
  122.5 22.0 %collective-permute-start.18 = (bf16[2048,256]{1,0:T(8,128)(2,1)}, bf16[2048,256]{1,0:T(8,128)(2,1)S(1)}, u32[]{:S(2)}, u32[]{:S(2)}) collective-permute-start(bf16[2048,256]{1,0:T(8,128)(2,1)} %take_states.13), channel_id=1, source_target_pairs={{0,8},{8,16},{16,24},{12,4},{20,12},{28,20},{1,9},{9,17},{17,25},{... | collective-permute-start | bytes 3145736 | tf_op jit(solution)/shard_map/ppermute | solution.py:908
  140.2 18.8 %collective-permute-start.19 = (bf16[2048,256]{1,0:T(8,128)(2,1)}, bf16[2048,256]{1,0:T(8,128)(2,1)S(1)}, u32[]{:S(2)}, u32[]{:S(2)}) collective-permute-start(bf16[2048,256]{1,0:T(8,128)(2,1)} %take_states.14), channel_id=1, source_target_pairs={{0,8},{8,16},{16,24},{12,4},{20,12},{28,20},{1,9},{9,17},{17,25},{... | collective-permute-start | bytes 3145736 | tf_op jit(solution)/shard_map/ppermute | solution.py:908
  144.5 40.0 %copy-start.24 = (bf16[2048,256]{1,0:T(8,128)(2,1)}, bf16[2048,256]{1,0:T(8,128)(2,1)S(1)}, u32[]{:S(2)}) copy-start(bf16[2048,256]{1,0:T(8,128)(2,1)S(1)} %collective-permute-done.18.rest_3_.rest_5_) | copy-start | bytes 3145732
  145.1 21.8 %collective-permute-start.20 = (bf16[2048,256]{1,0:T(8,128)(2,1)}, bf16[2048,256]{1,0:T(8,128)(2,1)}, u32[]{:S(2)}, u32[]{:S(2)}) collective-permute-start(bf16[2048,256]{1,0:T(8,128)(2,1)} %take_states.15), channel_id=1, source_target_pairs={{0,8},{8,16},{16,24},{12,4},{20,12},{28,20},{1,9},{9,17},{17,25},{... | collective-permute-start | bytes 3145736 | tf_op jit(solution)/shard_map/ppermute | solution.py:908
  159.0 25.5 %copy-start.26 = (bf16[2048,256]{1,0:T(8,128)(2,1)}, bf16[2048,256]{1,0:T(8,128)(2,1)S(1)}, u32[]{:S(2)}) copy-start(bf16[2048,256]{1,0:T(8,128)(2,1)S(1)} %collective-permute-done.19.rest_4_.rest_6_) | copy-start | bytes 3145732
  159.7 24.8 %collective-permute-start.21 = (bf16[2048,256]{1,0:T(8,128)(2,1)}, bf16[2048,256]{1,0:T(8,128)(2,1)}, u32[]{:S(2)}, u32[]{:S(2)}) collective-permute-start(bf16[2048,256]{1,0:T(8,128)(2,1)} %take_states.16), channel_id=1, source_target_pairs={{0,8},{8,16},{16,24},{12,4},{20,12},{28,20},{1,9},{9,17},{17,25},{... | collective-permute-start | bytes 3145736 | tf_op jit(solution)/shard_map/ppermute | solution.py:908
  167.6 31.5 %collective-permute-start.22 = (bf16[2048,256]{1,0:T(8,128)(2,1)}, bf16[2048,256]{1,0:T(8,128)(2,1)}, u32[]{:S(2)}, u32[]{:S(2)}) collective-permute-start(bf16[2048,256]{1,0:T(8,128)(2,1)} %take_states.17), channel_id=1, source_target_pairs={{0,8},{8,16},{16,24},{12,4},{20,12},{28,20},{1,9},{9,17},{17,25},{... | collective-permute-start | bytes 3145736 | tf_op jit(solution)/shard_map/ppermute | solution.py:908
  185.2 15.5 %collective-permute-start.23 = (bf16[2048,256]{1,0:T(8,128)(2,1)}, bf16[2048,256]{1,0:T(8,128)(2,1)}, u32[]{:S(2)}, u32[]{:S(2)}) collective-permute-start(bf16[2048,256]{1,0:T(8,128)(2,1)} %take_states.18), channel_id=1, source_target_pairs={{0,8},{8,16},{16,24},{12,4},{20,12},{28,20},{1,9},{9,17},{17,25},{... | collective-permute-start | bytes 3145736 | tf_op jit(solution)/shard_map/ppermute | solution.py:908
  188.2 0.9 copy-start.7
  201.3 6.8 %copy-start.2 = (bf16[1024,2048]{1,0:T(8,128)(2,1)S(1)}, bf16[1024,2048]{1,0:T(8,128)(2,1)}, u32[]{:S(2)}) copy-start(bf16[1024,2048]{1,0:T(8,128)(2,1)} %get-tuple-element.142.rest_15_) | copy-start | bytes 12582916
  201.3 6.8 %copy-start.5 = (bf16[1024,256]{1,0:T(8,128)(2,1)S(1)}, bf16[1024,256]{1,0:T(8,128)(2,1)}, u32[]{:S(2)}) copy-start(bf16[1024,256]{1,0:T(8,128)(2,1)} %get-tuple-element.176.c_ref.rest_13_) | copy-start | bytes 1572868
  201.3 6.8 %copy-start.10 = (bf16[128,2048]{1,0:T(8,128)(2,1)S(1)}, bf16[128,2048]{1,0:T(8,128)(2,1)}, u32[]{:S(2)}) copy-start(bf16[128,2048]{1,0:T(8,128)(2,1)} %constant.89.clone.spread_ref.rest_17_) | copy-start | bytes 1572868
  201.3 6.7 %copy-start.12 = (bf16[1024,128]{1,0:T(8,128)(2,1)S(1)}, bf16[1024,128]{1,0:T(8,128)(2,1)}, u32[]{:S(2)}) copy-start(bf16[1024,128]{1,0:T(8,128)(2,1)} %copy-done.11) | copy-start | bytes 786436
  201.3 6.7 %copy-start.19 = (f32[16,128]{1,0:T(8,128)S(1)}, f32[16,128]{1,0:T(8,128)}, u32[]{:S(2)}) copy-start(f32[16,128]{1,0:T(8,128)} %copy-done.18) | copy-start | bytes 24580
  201.3 6.7 %copy-start.20 = (f32[2048]{0:T(1024)S(1)}, f32[2048]{0:T(1024)}, u32[]{:S(2)}) copy-start(f32[2048]{0:T(1024)} %param.29) | copy-start | bytes 24580
  202.1 12.9 %collective-permute-start.24 = (bf16[4,2048,256]{2,1,0:T(8,128)(2,1)}, bf16[4,2048,256]{2,1,0:T(8,128)(2,1)S(1)}, u32[]{:S(2)}, u32[]{:S(2)}) collective-permute-start(bf16[4,2048,256]{2,1,0:T(8,128)(2,1)} %pick_states.1), channel_id=1, source_target_pairs={{0,4},{4,0},{8,12},{12,8},{16,20},{20,16},{24,28},{28,24},{1,5},{5... | collective-permute-start | bytes 12582920 | tf_op jit(solution)/shard_map/ppermute | solution.py:1039
  208.1 7.0 %copy-start.23 = (bf16[4,2048,256]{2,1,0:T(8,128)(2,1)S(1)}, bf16[4,2048,256]{2,1,0:T(8,128)(2,1)}, u32[]{:S(2)}) copy-start(bf16[4,2048,256]{2,1,0:T(8,128)(2,1)} %get-tuple-element.339) | copy-start | bytes 12582916
  208.1 7.0 %copy-start.25 = (bf16[2048,256]{1,0:T(8,128)(2,1)S(1)}, bf16[2048,256]{1,0:T(8,128)(2,1)}, u32[]{:S(2)}) copy-start(bf16[2048,256]{1,0:T(8,128)(2,1)} %get-tuple-element.341) | copy-start | bytes 3145732
  215.1 11.4 %copy-start.1 = (bf16[1024,2,4,128]{3,2,1,0:T(4,128)(2,1)S(1)}, bf16[1024,2,4,128]{3,2,1,0:T(4,128)(2,1)}, u32[]{:S(2)}) copy-start(bf16[1024,2,4,128]{3,2,1,0:T(4,128)(2,1)} %param.26) | copy-start | bytes 6291460
